TPU v7x, 32 devices: a whole 2x2x4 slice. The times are simulated.
32 devices in a mesh: section: 2 (over core), ctx: 4 (over y, x), tp: 4 (over z).
Axes of the slice: x: 2, y: 2, z: 4, core: 2. Of those that a mesh axis runs over, the one named last changes fastest.
Arguments:
- layer_inputs: bfloat16 [2, 6, 2, 1024, 1024], P('section', None, None, ('ctx', 'tp')), may hold values from -6 to 6
- out_grad: bfloat16 [6, 2, 1024, 1024], P(None, None, ('ctx', 'tp')), may hold values from -6 to 6
- src_seg: int32 [6, 2, 1024], P(None, None, 'ctx'), may hold values from 0 to 3, as said below
- tgt_seg: int32 [6, 2, 1024], P(None, None, 'ctx'), may hold values from 0 to 3, as said below
- qkv_weights: bfloat16 [2, 3, 1024, 1024], P('section', None, None, 'tp'), may hold values from -0.1875 to 0.1875
- out_weights: bfloat16 [2, 1024, 1024], P('section', None, 'tp'), may hold values from -0.75 to 0.75
- cross_weights: bfloat16 [2, 2, 1024, 1024], P('section', None, None, 'tp'), may hold values from -0.5 to 0.5, as said below
- ffn_in: bfloat16 [2, 1024, 4096], P('section', None, 'tp'), may hold values from -0.1875 to 0.1875
- ffn_out: bfloat16 [2, 4096, 1024], P('section', 'tp'), may hold values from -0.09375 to 0.09375
- adapter_in: bfloat16 [2, 1024, 512], P('section', None, 'tp'), may hold values from -0.1875 to 0.1875
- adapter_in_bias: bfloat16 [2, 512], P('section', 'tp'), may hold values from -4 to 4
- adapter_out: bfloat16 [2, 512, 1024], P('section', 'tp'), may hold values from -0.0625 to 0.0625
- adapter_out_bias: bfloat16 [2, 1024], P('section'), may hold values from -0.875 to 0.875
Outputs:
- layer_outputs: bfloat16 [2, 6, 2, 1024, 1024], P('section', None, None, ('ctx', 'tp'))
- input_grads: float32 [2, 6, 2, 1024, 1024], P('section', None, None, ('ctx', 'tp'))
- adapter_in_grad: float32 [2, 1024, 512], P('section', None, 'tp')
- adapter_in_bias_grad: float32 [2, 512], P('section', 'tp')
- adapter_out_grad: float32 [2, 512, 1024], P('section', 'tp')
- adapter_out_bias_grad: float32 [2, 1024], P('section')
Inputs may be any that keep to these rules, and one draw needn't show every extreme that they name: Along each row the ids never fall. In every micro-batch one row, drawn, holds the single id 0 in both src_seg and tgt_seg; every other row holds each of the ids 0 to 3 in both arrays. Every id of a row of tgt_seg also appears in the same row of src_seg, and the reverse. `cross_weights`: independent entries of mean zero.
All inputs are finite; a program needn't handle non-finite values.
Results may differ from a plain program's by a relative error of at most 0.022.
Values may be sent and summed in bfloat16 or wider, within the bound.
A program may use at most 576 MiB of HBM per device.

v0:
```python
import jax
import jax.numpy as jnp
from jax import lax
from jax.sharding import PartitionSpec as P

HEAD = 64


eps = 1e-05
masked = -1e30


def partner(value, axis, stride):
    mask = 2**stride
    pairs = [(source, source ^ mask) for source in range(lax.axis_size(axis))]
    return lax.ppermute(value, axis, pairs)


def layer_norm(tensor):
    row_mean = jnp.mean(tensor, axis=-1, keepdims=True)
    centered = tensor - row_mean
    return centered * lax.rsqrt(jnp.mean(centered * centered, axis=-1, keepdims=True) + eps)


def norm_back(tensor, upstream):
    return jax.vjp(layer_norm, tensor)[1](upstream)[0]


def gelu_exact(tensor):
    return jax.nn.gelu(tensor, approximate=False)


def forward_dot(operand, matrix):
    return jnp.einsum("rpk,km->rpm", operand, matrix, preferred_element_type=jnp.float32)


def backward_dot(operand, matrix):
    return jnp.einsum("rpm,km->rpk", operand, matrix, preferred_element_type=jnp.float32)


def weight_grad(operand, upstream):
    return jnp.einsum("rpk,rpm->km", operand, upstream, preferred_element_type=jnp.float32)


def split_heads(tensor):
    return tensor.reshape(tensor.shape[0], tensor.shape[1], tensor.shape[2] // HEAD, HEAD)


def join_heads(tensor):
    return tensor.reshape(tensor.shape[0], tensor.shape[1], tensor.shape[2] * tensor.shape[3])


def positions(length):
    return lax.axis_index("ctx") * length + jnp.arange(length, dtype=jnp.int32)


def allowed_mask(seg_query, seg_key, pos_query, pos_key, causal):
    allowed = seg_query[:, :, None] == seg_key[:, None, :]
    if causal:
        allowed = allowed & (pos_query[None, :, None] >= pos_key[None, None, :])
    return allowed[:, None]


def raw_scores(queries, keys_all, allowed):
    scores = jnp.einsum(
        "rqhd,rkhd->rhqk",
        split_heads(queries),
        split_heads(keys_all),
        preferred_element_type=jnp.float32,
    )
    return jnp.where(allowed, scores * HEAD ** (-0.5), masked)


def block_gather(tensor):
    return lax.all_gather(tensor, "tp", axis=1, tiled=True)


def block_sum(tensor):
    return lax.psum_scatter(
        tensor.astype(jnp.bfloat16), "tp", scatter_dimension=1, tiled=True
    ).astype(jnp.float32)


def gather_keys(keys_own, values_own, segments):
    return (
        lax.all_gather(keys_own, "ctx", axis=1, tiled=True),
        lax.all_gather(values_own, "ctx", axis=1, tiled=True),
        lax.all_gather(segments, "ctx", axis=1, tiled=True),
    )


def attend_forward(queries, keys_all, values_all, allowed):
    scores = raw_scores(queries, keys_all, allowed)
    row_max = jnp.max(scores, axis=-1, keepdims=True)
    log_total = row_max + jnp.log(jnp.sum(jnp.exp(scores - row_max), axis=-1, keepdims=True))
    soft_weights = jnp.exp(scores - log_total)
    attn_out = jnp.einsum(
        "rhqk,rkhd->rqhd",
        soft_weights.astype(jnp.bfloat16),
        split_heads(values_all),
        preferred_element_type=jnp.float32,
    )
    return (join_heads(attn_out).astype(jnp.bfloat16), log_total)


def attention_backward(queries, keys_all, values_all, allowed, log_total, grad_attn):
    head_scale = HEAD ** (-0.5)
    soft_weights = jnp.exp(raw_scores(queries, keys_all, allowed) - log_total)
    grad_weights = jnp.einsum(
        "rqhd,rkhd->rhqk",
        split_heads(grad_attn),
        split_heads(values_all),
        preferred_element_type=jnp.float32,
    )
    row_delta = jnp.sum(soft_weights * grad_weights, axis=-1, keepdims=True)
    grad_scores = (soft_weights * (grad_weights - row_delta)).astype(jnp.bfloat16)
    grad_query = (
        join_heads(
            jnp.einsum(
                "rhqk,rkhd->rqhd",
                grad_scores,
                split_heads(keys_all),
                preferred_element_type=jnp.float32,
            )
        )
        * head_scale
    )
    key_terms = (
        join_heads(
            jnp.einsum(
                "rhqk,rqhd->rkhd",
                grad_scores,
                split_heads(queries),
                preferred_element_type=jnp.float32,
            )
        )
        * head_scale
    )
    value_terms = join_heads(
        jnp.einsum(
            "rhqk,rqhd->rkhd",
            soft_weights.astype(jnp.bfloat16),
            split_heads(grad_attn),
            preferred_element_type=jnp.float32,
        )
    )
    grad_keys, grad_values = (
        lax.psum_scatter(
            key_terms.astype(jnp.bfloat16), "ctx", scatter_dimension=1, tiled=True
        ).astype(jnp.float32),
        lax.psum_scatter(
            value_terms.astype(jnp.bfloat16), "ctx", scatter_dimension=1, tiled=True
        ).astype(jnp.float32),
    )
    return (grad_query, grad_keys, grad_values)


def self_forward(inputs, segments, w_qkv, w_out, causal):
    row_block = block_gather(inputs.astype(jnp.bfloat16))
    projected = jnp.einsum(
        "rpk,jkm->jrpm", row_block, w_qkv, preferred_element_type=jnp.float32
    ).astype(jnp.bfloat16)
    queries, keys_own, values_own = (projected[0], projected[1], projected[2])
    keys_all, values_all, key_seg = gather_keys(keys_own, values_own, segments)
    allowed = allowed_mask(
        segments,
        key_seg,
        positions(segments.shape[1]),
        jnp.arange(key_seg.shape[1], dtype=jnp.int32),
        causal,
    )
    attn_out, log_total = attend_forward(queries, keys_all, values_all, allowed)
    pre_norm = inputs + block_sum(backward_dot(attn_out, w_out))
    kept_attn = (queries, keys_own, values_own, keys_all, values_all, allowed, log_total)
    return (layer_norm(pre_norm), pre_norm, kept_attn)


def self_backward(grad_norm, pre_norm, kept_attn, w_qkv, w_out):
    queries, keys_own, values_own, keys_all, values_all, allowed, log_total = kept_attn
    grad_pre = norm_back(pre_norm, grad_norm)
    grad_block = block_gather(grad_pre.astype(jnp.bfloat16))
    grad_attn = forward_dot(grad_block, w_out).astype(jnp.bfloat16)
    grad_query, grad_keys, grad_values = attention_backward(
        queries, keys_all, values_all, allowed, log_total, grad_attn
    )
    stacked = jnp.stack([grad_query, grad_keys, grad_values]).astype(jnp.bfloat16)
    grad_rows = jnp.einsum("jrpm,jkm->rpk", stacked, w_qkv, preferred_element_type=jnp.float32)
    return block_sum(grad_rows) + grad_pre


def tail_forward(hidden, tail_w):
    w_in, w_out, a_in, b_in, a_out, b_out = tail_w
    row_block = block_gather(hidden.astype(jnp.bfloat16))
    inner_act = forward_dot(row_block, w_in)
    gelu_out = gelu_exact(inner_act).astype(jnp.bfloat16)
    adapter_pre = forward_dot(row_block, a_in) + b_in.astype(jnp.float32)
    gated_act = jax.nn.silu(adapter_pre).astype(jnp.bfloat16)
    partial_sum = forward_dot(gelu_out, w_out) + 4.0 * forward_dot(gated_act, a_out)
    pre_norm = hidden + block_sum(partial_sum) + 4.0 * b_out.astype(jnp.float32)
    return (layer_norm(pre_norm), pre_norm, (row_block, inner_act, adapter_pre, gated_act))


def tail_backward(grad_norm, pre_norm, kept_tail, tail_w):
    w_in, w_out, a_in, b_in, a_out, b_out = tail_w
    row_block, inner_act, adapter_pre, gated_act = kept_tail
    grad_pre = norm_back(pre_norm, grad_norm)
    grad_branch = block_gather(grad_pre.astype(jnp.bfloat16))
    grad_inner = jax.vjp(gelu_exact, inner_act)[1](backward_dot(grad_branch, w_out))[0].astype(
        jnp.bfloat16
    )
    grad_adapter = jax.vjp(jax.nn.silu, adapter_pre)[1](4.0 * backward_dot(grad_branch, a_out))[
        0
    ].astype(jnp.bfloat16)
    adapter_terms = (
        weight_grad(row_block, grad_adapter),
        jnp.sum(grad_adapter.astype(jnp.float32), axis=(0, 1)),
        4.0 * weight_grad(gated_act, grad_branch),
        4.0 * jnp.sum(grad_branch.astype(jnp.float32), axis=(0, 1)),
    )
    grad_rows = backward_dot(grad_inner, w_in) + backward_dot(grad_adapter, a_in)
    return (block_sum(grad_rows) + grad_pre, adapter_terms)


def encoder_forward(source, segments, weights):
    w_qkv, w_out, w_cross, tail_w = weights
    mid_norm, pre_self, kept_self = self_forward(source, segments, w_qkv, w_out, False)
    encoded, pre_tail, kept_tail = tail_forward(mid_norm, tail_w)
    return (encoded, (pre_self, kept_self, pre_tail, kept_tail))


def empty_kept(inputs, qkv_weights, ffn_in, adapter_in):
    row_count = inputs.shape[1]
    own_part = inputs.shape[2]
    width = inputs.shape[3]
    block_len = own_part * lax.axis_size("tp")
    total_len = block_len * lax.axis_size("ctx")
    head_cols = qkv_weights.shape[3]
    local_heads = head_cols // HEAD
    hidden_cols = ffn_in.shape[2]
    adapter_cols = adapter_in.shape[2]
    pre_zero = jnp.zeros((row_count, own_part, width), jnp.float32)
    own_zero = jnp.zeros((row_count, block_len, head_cols), jnp.bfloat16)
    all_zero = jnp.zeros((row_count, total_len, head_cols), jnp.bfloat16)
    kept_self = (
        own_zero,
        own_zero,
        own_zero,
        all_zero,
        all_zero,
        jnp.zeros((row_count, 1, block_len, total_len), jnp.bool_),
        jnp.zeros((row_count, local_heads, block_len, 1), jnp.float32),
    )
    kept_tail = (
        jnp.zeros((row_count, block_len, width), jnp.bfloat16),
        jnp.zeros((row_count, block_len, hidden_cols), jnp.float32),
        jnp.zeros((row_count, block_len, adapter_cols), jnp.float32),
        jnp.zeros((row_count, block_len, adapter_cols), jnp.bfloat16),
    )
    return (pre_zero, kept_self, pre_zero, kept_tail)


def encoder_memory(encoded, w_cross):
    row_block = block_gather(encoded.astype(jnp.bfloat16))
    memory = jnp.einsum(
        "rpk,jkm->rpjm", row_block, w_cross, preferred_element_type=jnp.float32
    ).astype(jnp.bfloat16)
    return memory.reshape(memory.shape[0], memory.shape[1], memory.shape[2] * memory.shape[3])


def encoder_backward(kept_all, weights, grad_memory):
    w_qkv, w_out, w_cross, tail_w = weights
    pre_self, kept_self, pre_tail, kept_tail = kept_all
    paired = grad_memory.reshape(
        grad_memory.shape[0], grad_memory.shape[1], 2, grad_memory.shape[2] // 2
    )
    grad_encoded = block_sum(
        jnp.einsum("rpjm,jkm->rpk", paired, w_cross, preferred_element_type=jnp.float32)
    )
    grad_mid, adapter_terms = tail_backward(grad_encoded, pre_tail, kept_tail, tail_w)
    return (self_backward(grad_mid, pre_self, kept_self, w_qkv, w_out), adapter_terms)


def decoder_step(target, seg_target, seg_source, memory, cotangent, weights):
    w_qkv, w_out, w_cross, tail_w = weights
    width = w_qkv.shape[2]
    first_norm, pre_self, kept_self = self_forward(target, seg_target, w_qkv, w_out, True)
    row_block = block_gather(first_norm.astype(jnp.bfloat16))
    queries = forward_dot(row_block, w_cross[0]).astype(jnp.bfloat16)
    mem_keys = memory[..., :width]
    mem_values = memory[..., width:]
    keys_all, values_all, key_seg = gather_keys(mem_keys, mem_values, seg_source)
    allowed = allowed_mask(
        seg_target,
        key_seg,
        positions(seg_target.shape[1]),
        jnp.arange(key_seg.shape[1], dtype=jnp.int32),
        False,
    )
    attn_out, log_total = attend_forward(queries, keys_all, values_all, allowed)
    pre_cross = first_norm + block_sum(backward_dot(attn_out, w_cross[1]))
    second_norm = layer_norm(pre_cross)
    decoded, pre_tail, kept_tail = tail_forward(second_norm, tail_w)
    grad_second, adapter_terms = tail_backward(cotangent, pre_tail, kept_tail, tail_w)
    grad_cross = norm_back(pre_cross, grad_second)
    grad_block = block_gather(grad_cross.astype(jnp.bfloat16))
    grad_attn = forward_dot(grad_block, w_cross[1]).astype(jnp.bfloat16)
    grad_query, grad_keys, grad_values = attention_backward(
        queries, keys_all, values_all, allowed, log_total, grad_attn
    )
    grad_memory = jnp.concatenate([grad_keys, grad_values], axis=-1).astype(jnp.bfloat16)
    grad_first = block_sum(backward_dot(grad_query.astype(jnp.bfloat16), w_cross[0])) + grad_cross
    grad_target = self_backward(grad_first, pre_self, kept_self, w_qkv, w_out)
    return (decoded, grad_target, grad_memory, adapter_terms)


def per_device(
    layer_inputs,
    out_grad,
    src_seg,
    tgt_seg,
    qkv_weights,
    out_weights,
    cross_weights,
    ffn_in,
    ffn_out,
    adapter_in,
    adapter_in_bias,
    adapter_out,
    adapter_out_bias,
):
    inputs = layer_inputs[0]
    micro_count = inputs.shape[0]
    tail_w = (
        ffn_in[0],
        ffn_out[0],
        adapter_in[0],
        adapter_in_bias[0],
        adapter_out[0],
        adapter_out_bias[0],
    )
    weights = (qkv_weights[0], out_weights[0], cross_weights[0], tail_w)
    is_first = lax.axis_index("section") == 0
    outs_buf = jnp.zeros(inputs.shape, jnp.bfloat16)
    grads_buf = jnp.zeros(inputs.shape, jnp.float32)
    totals = (
        jnp.zeros(adapter_in[0].shape, jnp.float32),
        jnp.zeros(adapter_in_bias[0].shape, jnp.float32),
        jnp.zeros(adapter_out[0].shape, jnp.float32),
        jnp.zeros(adapter_out_bias[0].shape, jnp.float32),
    )
    handoff_shape = (inputs.shape[1], src_seg.shape[2], 2 * qkv_weights.shape[3])
    received = jnp.zeros(handoff_shape, jnp.bfloat16)
    blank = empty_kept(inputs, qkv_weights, ffn_in, adapter_in)
    slots = (blank, blank, blank)

    def pick(first_value, second_value):
        return jnp.where(is_first, first_value, second_value)

    for tick_index in range(micro_count + 2):
        carried = (outs_buf, grads_buf, totals, received, slots)
        outs_enc, grads_enc, totals_enc, incoming, slots_now = carried
        slot_list = list(slots_now)
        out_enc = jnp.zeros(handoff_shape, jnp.bfloat16)
        if tick_index < micro_count:
            encoded, kept_now = encoder_forward(
                inputs[tick_index].astype(jnp.float32), src_seg[tick_index], weights
            )
            outs_enc = outs_enc.at[tick_index].set(encoded.astype(jnp.bfloat16))
            out_enc = encoder_memory(encoded, weights[2])
            slot_list[tick_index % 3] = kept_now
        if tick_index >= 2:
            earlier = tick_index - 2
            grad_source, enc_terms = encoder_backward(slot_list[earlier % 3], weights, incoming)
            grads_enc = grads_enc.at[earlier].set(grad_source)
            totals_enc = jax.tree.map(jnp.add, totals_enc, enc_terms)
        outs_dec, grads_dec, totals_dec = (outs_buf, grads_buf, totals)
        out_dec = jnp.zeros(handoff_shape, jnp.bfloat16)
        current = tick_index - 1
        if 0 <= current < micro_count:
            decoded, grad_target, grad_memory, dec_terms = decoder_step(
                inputs[current].astype(jnp.float32),
                tgt_seg[current],
                src_seg[current],
                received,
                out_grad[current].astype(jnp.float32),
                weights,
            )
            outs_dec = outs_dec.at[current].set(decoded.astype(jnp.bfloat16))
            grads_dec = grads_dec.at[current].set(grad_target)
            totals_dec = jax.tree.map(jnp.add, totals_dec, dec_terms)
            out_dec = grad_memory
        outs_buf = pick(outs_enc, outs_dec)
        grads_buf = pick(grads_enc, grads_dec)
        totals = jax.tree.map(pick, totals_enc, totals_dec)
        outgoing = pick(out_enc, out_dec)
        slots = tuple(slot_list)
        if tick_index <= micro_count:
            received = partner(outgoing, "section", 0)
    summed = (
        lax.psum(totals[0].astype(jnp.bfloat16), "ctx").astype(jnp.float32),
        lax.psum(totals[1].astype(jnp.bfloat16), "ctx").astype(jnp.float32),
        lax.psum(totals[2].astype(jnp.bfloat16), "ctx").astype(jnp.float32),
        lax.psum(totals[3].astype(jnp.bfloat16), "ctx").astype(jnp.float32),
    )
    return (
        outs_buf[None],
        grads_buf[None],
        summed[0][None],
        summed[1][None],
        summed[2][None],
        summed[3][None],
    )


def solution(mesh):
    return jax.shard_map(
        per_device,
        mesh=mesh,
        in_specs=(
            P("section", None, None, ("ctx", "tp"), None),
            P(None, None, ("ctx", "tp"), None),
            P(None, None, "ctx"),
            P(None, None, "ctx"),
            P("section", None, None, "tp"),
            P("section", None, "tp"),
            P("section", None, None, "tp"),
            P("section", None, "tp"),
            P("section", "tp", None),
            P("section", None, "tp"),
            P("section", "tp"),
            P("section", "tp", None),
            P("section", None),
        ),
        out_specs=(
            P("section", None, None, ("ctx", "tp"), None),
            P("section", None, None, ("ctx", "tp"), None),
            P("section", None, "tp"),
            P("section", "tp"),
            P("section", "tp", None),
            P("section", None),
        ),
        check_vma=False,
    )
```

profile of v0, /device:TPU:0, one launch (start us, length us, event | category | flops | bytes accessed | tf_op | source)
XLA Modules:
  0.0 5703.4 jit_solution(13430366022958219492)
XLA Ops:
  556.2 28.1 reduce-scatter.121.cloned.1.call-done
  584.3 28.1 reduce-scatter.153.cloned.1.call-done
  612.4 28.2 reduce-scatter.111.cloned.1.call-done
  668.8 28.1 reduce-scatter.107.cloned.1.call-done
  696.9 28.7 reduce-scatter.133.cloned.1.call-done
  725.5 28.1 reduce-scatter.181.cloned.1.call-done
  1275.3 28.2 reduce-scatter.135.cloned.1.call-done
  1418.9 30.5 reduce-scatter.125.cloned.1.call-done
  1803.1 30.9 reduce-scatter.141.cloned.1.call-done
  2187.3 30.5 reduce-scatter.157.cloned.1.call-done
  2610.1 28.1 reduce-scatter.247.cloned.1.call-done
  2742.3 28.1 reduce-scatter.175.cloned.1.call-done
  2770.4 30.5 reduce-scatter.173.cloned.1.call-done
  2895.2 28.2 reduce-scatter.257.cloned.1.call-done
  3290.4 28.0 reduce-scatter.221.cloned.1.call-done
  3318.4 28.7 reduce-scatter.265.cloned.1.call-done
  3449.6 28.5 reduce-scatter.187.cloned.1.call-done
  3478.0 30.7 reduce-scatter.185.cloned.1.call-done
  3603.0 28.0 reduce-scatter.275.cloned.1.call-done
  3987.9 30.7 reduce-scatter.293.cloned.1.call-done
  4138.1 28.0 reduce-scatter.285.cloned.1.call-done
  4194.3 28.2 reduce-scatter.299.cloned.1.call-done
  4783.8 30.9 reduce-scatter.223.cloned.1.call-done
  4845.4 30.9 reduce-scatter.231.cloned.1.call-done
  4906.9 30.9 reduce-scatter.241.cloned.1.call-done
  4968.3 30.9 reduce-scatter.249.cloned.1.call-done
  5029.7 30.8 reduce-scatter.259.cloned.1.call-done
  5091.0 30.9 reduce-scatter.267.cloned.1.call-done
  5152.4 30.9 reduce-scatter.277.cloned.1.call-done
  5214.0 30.7 reduce-scatter.287.cloned.1.call-done
  5263.5 30.4 all-reduce.6.cloned.1.call-done
  5324.6 30.8 reduce-scatter.301.cloned.1.call-done
  (2667 shorter events, 4734.3 us)
Async XLA Ops:
  4247.7 486.6 %reduce-scatter.197.cloned.1.call-start = ((), (), s32[]{:S(2)}) async-start(), calls=%async_computation.196 | async-start | bytes 1310720 | tf_op jit(solution)/shard_map/reduce_scatter | solution.py:151
  4325.6 408.7 %reduce-scatter.195.cloned.1.call-start = ((), (), s32[]{:S(2)}) async-start(), calls=%async_computation.195 | async-start | bytes 1310720 | tf_op jit(solution)/shard_map/reduce_scatter | solution.py:148
  4376.7 365.9 %reduce-scatter.207.cloned.1.call-start = ((), (), s32[]{:S(2)}) async-start(), calls=%async_computation.203 | async-start | bytes 1310720 | tf_op jit(solution)/shard_map/reduce_scatter | solution.py:151
  4392.6 358.3 %reduce-scatter.215.cloned.1.call-start = ((), (), s32[]{:S(2)}) async-start(), calls=%async_computation.208 | async-start | bytes 1310720 | tf_op jit(solution)/shard_map/reduce_scatter | solution.py:151
  4449.5 365.2 %reduce-scatter.223.cloned.1.call-start = ((), (), s32[]{:S(2)}) async-start(), calls=%async_computation.214 | async-start | bytes 1310720 | tf_op jit(solution)/shard_map/reduce_scatter | solution.py:148
  4464.7 380.7 %reduce-scatter.233.cloned.1.call-start = ((), (), s32[]{:S(2)}) async-start(), calls=%async_computation.220 | async-start | bytes 1310720 | tf_op jit(solution)/shard_map/reduce_scatter | solution.py:151
  4574.7 363.1 %reduce-scatter.241.cloned.1.call-start = ((), (), s32[]{:S(2)}) async-start(), calls=%async_computation.226 | async-start | bytes 1310720 | tf_op jit(solution)/shard_map/reduce_scatter | solution.py:148
  4581.1 387.3 %reduce-scatter.251.cloned.1.call-start = ((), (), s32[]{:S(2)}) async-start(), calls=%async_computation.232 | async-start | bytes 1310720 | tf_op jit(solution)/shard_map/reduce_scatter | solution.py:151
  4598.3 400.9 %reduce-scatter.249.cloned.1.call-start = ((), (), s32[]{:S(2)}) async-start(), calls=%async_computation.231 | async-start | bytes 1310720 | tf_op jit(solution)/shard_map/reduce_scatter | solution.py:148
  4628.3 401.5 %reduce-scatter.261.cloned.1.call-start = ((), (), s32[]{:S(2)}) async-start(), calls=%async_computation.239 | async-start | bytes 1310720 | tf_op jit(solution)/shard_map/reduce_scatter | solution.py:151
  4637.6 422.9 %reduce-scatter.259.cloned.1.call-start = ((), (), s32[]{:S(2)}) async-start(), calls=%async_computation.238 | async-start | bytes 1310720 | tf_op jit(solution)/shard_map/reduce_scatter | solution.py:148
  4644.1 446.9 %reduce-scatter.269.cloned.1.call-start = ((), (), s32[]{:S(2)}) async-start(), calls=%async_computation.244 | async-start | bytes 1310720 | tf_op jit(solution)/shard_map/reduce_scatter | solution.py:151
  4653.3 468.6 %reduce-scatter.267.cloned.1.call-start = ((), (), s32[]{:S(2)}) async-start(), calls=%async_computation.243 | async-start | bytes 1310720 | tf_op jit(solution)/shard_map/reduce_scatter | solution.py:148
  4659.9 492.5 %reduce-scatter.279.cloned.1.call-start = ((), (), s32[]{:S(2)}) async-start(), calls=%async_computation.251 | async-start | bytes 1310720 | tf_op jit(solution)/shard_map/reduce_scatter | solution.py:151
  4669.0 514.3 %reduce-scatter.277.cloned.1.call-start = ((), (), s32[]{:S(2)}) async-start(), calls=%async_computation.250 | async-start | bytes 1310720 | tf_op jit(solution)/shard_map/reduce_scatter | solution.py:148
  4679.6 534.4 %reduce-scatter.289.cloned.1.call-start = ((), (), s32[]{:S(2)}) async-start(), calls=%async_computation.259 | async-start | bytes 1310720 | tf_op jit(solution)/shard_map/reduce_scatter | solution.py:151
  4694.8 549.9 %reduce-scatter.287.cloned.1.call-start = ((), (), s32[]{:S(2)}) async-start(), calls=%async_computation.258 | async-start | bytes 1310720 | tf_op jit(solution)/shard_map/reduce_scatter | solution.py:148
  4706.7 587.3 %all-reduce.6.cloned.1.call-start = ((), (), s32[]{:S(2)}) async-start(), calls=%async_computation.288 | async-start | bytes 1048576 | tf_op jit(solution)/shard_map/psum | solution.py:400
  4715.5 609.1 %reduce-scatter.303.cloned.1.call-start = ((), (), s32[]{:S(2)}) async-start(), calls=%async_computation.268 | async-start | bytes 1310720 | tf_op jit(solution)/shard_map/reduce_scatter | solution.py:151
  4725.0 630.3 %reduce-scatter.301.cloned.1.call-start = ((), (), s32[]{:S(2)}) async-start(), calls=%async_computation.267 | async-start | bytes 1310720 | tf_op jit(solution)/shard_map/reduce_scatter | solution.py:148
  4729.5 655.9 %reduce-scatter.199.cloned.1.call-start = ((), (), s32[]{:S(2)}) async-start(), calls=%async_computation.197 | async-start | bytes 1310720 | tf_op jit(solution)/shard_map/reduce_scatter | solution.py:79
  4738.0 675.4 %reduce-scatter.209.cloned.1.call-start = ((), (), s32[]{:S(2)}) async-start(), calls=%async_computation.204 | async-start | bytes 1310720 | tf_op jit(solution)/shard_map/reduce_scatter | solution.py:79
  4746.3 695.1 %reduce-scatter.217.cloned.1.call-start = ((), (), s32[]{:S(2)}) async-start(), calls=%async_computation.209 | async-start | bytes 1310720 | tf_op jit(solution)/shard_map/reduce_scatter | solution.py:79
  4756.8 712.7 %reduce-scatter.227.cloned.1.call-start = ((), (), s32[]{:S(2)}) async-start(), calls=%async_computation.216 | async-start | bytes 1310720 | tf_op jit(solution)/shard_map/reduce_scatter | solution.py:79
  4818.5 679.1 %reduce-scatter.235.cloned.1.call-start = ((), (), s32[]{:S(2)}) async-start(), calls=%async_computation.221 | async-start | bytes 1310720 | tf_op jit(solution)/shard_map/reduce_scatter | solution.py:79
  4880.1 645.8 %reduce-scatter.245.cloned.1.call-start = ((), (), s32[]{:S(2)}) async-start(), calls=%async_computation.228 | async-start | bytes 1310720 | tf_op jit(solution)/shard_map/reduce_scatter | solution.py:79
  4941.6 612.4 %reduce-scatter.253.cloned.1.call-start = ((), (), s32[]{:S(2)}) async-start(), calls=%async_computation.233 | async-start | bytes 1310720 | tf_op jit(solution)/shard_map/reduce_scatter | solution.py:79
  5003.0 579.1 %reduce-scatter.263.cloned.1.call-start = ((), (), s32[]{:S(2)}) async-start(), calls=%async_computation.240 | async-start | bytes 1310720 | tf_op jit(solution)/shard_map/reduce_scatter | solution.py:79
  5064.3 545.8 %reduce-scatter.271.cloned.1.call-start = ((), (), s32[]{:S(2)}) async-start(), calls=%async_computation.245 | async-start | bytes 1310720 | tf_op jit(solution)/shard_map/reduce_scatter | solution.py:79
  5125.6 512.5 %reduce-scatter.281.cloned.1.call-start = ((), (), s32[]{:S(2)}) async-start(), calls=%async_computation.252 | async-start | bytes 1310720 | tf_op jit(solution)/shard_map/reduce_scatter | solution.py:79
  5186.9 479.3 %reduce-scatter.291.cloned.1.call-start = ((), (), s32[]{:S(2)}) async-start(), calls=%async_computation.260 | async-start | bytes 1310720 | tf_op jit(solution)/shard_map/reduce_scatter | solution.py:79
  5248.3 446.0 %reduce-scatter.305.cloned.1.call-start = ((), (), s32[]{:S(2)}) async-start(), calls=%async_computation.269 | async-start | bytes 1310720 | tf_op jit(solution)/shard_map/reduce_scatter | solution.py:79
  (866 other events, 41938.1 us)
Sparse Core Ops, SparseCore 0:
  10.2 30.6 all-gather.258
  1421.6 27.7 reduce-scatter.124
  1451.0 27.9 all-gather.138
  1835.5 27.9 all-gather.154
  2190.0 27.7 reduce-scatter.156
  2219.3 27.9 all-gather.170
  2773.1 27.7 reduce-scatter.172
  3481.0 27.7 reduce-scatter.184
  3990.8 27.7 reduce-scatter.292
  4020.1 27.9 all-gather.208
  4602.8 27.7 reduce-scatter.194
  4664.0 27.7 reduce-scatter.204
  4725.4 27.7 reduce-scatter.212
  4756.1 27.7 reduce-scatter.224
  4787.0 27.7 reduce-scatter.222
  4817.6 27.7 reduce-scatter.232
  4848.5 27.7 reduce-scatter.230
  4879.2 27.7 reduce-scatter.242
  4910.1 27.7 reduce-scatter.240
  4940.6 27.7 reduce-scatter.250
  4971.5 27.7 reduce-scatter.248
  5002.0 27.7 reduce-scatter.260
  5032.7 27.7 reduce-scatter.258
  5063.2 27.7 reduce-scatter.268
  5094.1 27.7 reduce-scatter.266
  5124.6 27.7 reduce-scatter.278
  5155.6 27.7 reduce-scatter.276
  5186.2 27.7 reduce-scatter.288
  5216.9 27.7 reduce-scatter.286
  5248.1 45.7 all-reduce.5
  5296.8 27.7 reduce-scatter.302
  5327.6 27.7 reduce-scatter.300
  (155 shorter events, 4113.5 us)
where the time goes:
time: 5720 us; the launch traced here: 5700 us
  waiting for transfers between devices  3950 us (69%)
  matrix products  1050 us (18%)
  other arithmetic  396 us (7%)
  local copies, waits for them, and re-layouts  155 us (3%)
  blocking collectives  101 us (2%)
    reduce_scatter x66, waiting for transfers between devices, block_sum(): lax.psum_scatter(tensor.astype(jnp.bfloat16), 'tp', scatter_dimension=1,...  1590 us
    all_gather x60, waiting for transfers between devices, block_gather(): return lax.all_gather(tensor, 'tp', axis=1, tiled=True)  1070 us
    reduce_scatter x18, waiting for transfers between devices, attention_backward(): lax.psum_scatter(key_terms.astype(jnp.bfloat16), 'ctx', scatter_dimension...  464 us
    reduce_scatter x18, waiting for transfers between devices, attention_backward(): lax.psum_scatter(value_terms.astype(jnp.bfloat16), 'ctx', scatter_dimensi...  362 us
    dot_general x60, matrix products, backward_dot(): jnp.einsum('rpm,km->rpk', operand, matrix, preferred_element_type=jnp.flo...  224 us
    all_gather x12, waiting for transfers between devices, gather_keys(): lax.all_gather(keys_own, 'ctx', axis=1, tiled=True)  208 us
    all_gather x12, waiting for transfers between devices, gather_keys(): lax.all_gather(values_own, 'ctx', axis=1, tiled=True)  203 us
    dot_general x72, matrix products, forward_dot(): jnp.einsum('rpk,km->rpm', operand, matrix, preferred_element_type=jnp.flo...  182 us
  transfers between devices with their start and end apart: 194, of which 179 were waited for; matrix products, arithmetic and copies ran while one was open for 22% of the time, Pallas kernels for 0%

commit v1 on v0

v1 whole, which is shorter than its diff:
```python
import functools

import jax
import jax.numpy as jnp
from jax import lax
from jax.experimental import pallas as pl
from jax.experimental.pallas import tpu as pltpu
from jax.sharding import PartitionSpec as P

HEAD = 64
SCALE = HEAD**-0.5
EPS = 1e-05
MASKED = -1e30
F32 = jnp.float32
BF16 = jnp.bfloat16


def swap(value):
    return lax.ppermute(value, "section", [(0, 1), (1, 0)])


def dot_nt(left, right, **kw):
    return lax.dot_general(
        left, right, (((1,), (1,)), ((), ())), preferred_element_type=F32, **kw
    )


def dot_nn(left, right):
    return lax.dot_general(
        left, right, (((1,), (0,)), ((), ())), preferred_element_type=F32
    )


def dot_tn(left, right):
    return lax.dot_general(
        left, right, (((0,), (0,)), ((), ())), preferred_element_type=F32
    )


def attn_fwd_kernel(
    causal, q_ref, ko_ref, kx_ref, vo_ref, vx_ref, qi_ref, ki_ref, o_ref, lse_ref
):
    length = q_ref.shape[1]
    heads = q_ref.shape[2] // HEAD
    block = length // 2
    segq = qi_ref[:, 0:1]
    posq = qi_ref[:, 1:2]
    for h in range(heads):
        cols = slice(h * HEAD, (h + 1) * HEAD)
        for b in range(2):
            rows = slice(b * block, (b + 1) * block)
            span = (b + 1) * block if causal else length
            q = q_ref[0, rows, cols] * jnp.asarray(SCALE, BF16)
            parts = []
            for kk, (k_ref, i) in enumerate(((ko_ref, 0), (kx_ref, 2))):
                s = dot_nt(q, k_ref[0, :span, cols])
                ok = segq[rows] == ki_ref[i : i + 1, :span]
                if causal:
                    ok = ok & (posq[rows] >= ki_ref[i + 1 : i + 2, :span])
                parts.append(jnp.where(ok, s, MASKED))
            top = jnp.maximum(
                jnp.max(parts[0], axis=1, keepdims=True),
                jnp.max(parts[1], axis=1, keepdims=True),
            )
            ex = [jnp.exp(p - top) for p in parts]
            total = jnp.sum(ex[0], axis=1, keepdims=True) + jnp.sum(
                ex[1], axis=1, keepdims=True
            )
            out = dot_nn(ex[0].astype(BF16), vo_ref[0, :span, cols]) + dot_nn(
                ex[1].astype(BF16), vx_ref[0, :span, cols]
            )
            o_ref[0, rows, cols] = (out / total).astype(BF16)
            lse = top + jnp.log(total)
            lse_ref[0, h : h + 1, rows] = jnp.broadcast_to(lse, (block, 128)).T[0:1]


def attention_forward(q, k_own, k_oth, v_own, v_oth, qi, ki, causal):
    groups, length, width = q.shape
    heads = width // HEAD
    spec = pl.BlockSpec((1, length, width), lambda t: (t, 0, 0))
    return pl.pallas_call(
        functools.partial(attn_fwd_kernel, causal),
        grid=(groups,),
        in_specs=[spec] * 5
        + [
            pl.BlockSpec(qi.shape, lambda t: (0, 0)),
            pl.BlockSpec(ki.shape, lambda t: (0, 0)),
        ],
        out_specs=[spec, pl.BlockSpec((1, heads, length), lambda t: (t, 0, 0))],
        out_shape=[
            jax.ShapeDtypeStruct(q.shape, BF16),
            jax.ShapeDtypeStruct((groups, heads, length), F32),
        ],
        compiler_params=pltpu.CompilerParams(vmem_limit_bytes=48 * 2**20),
        name="attn_fwd",
    )(q, k_own, k_oth, v_own, v_oth, qi, ki)


def attn_bwd_kernel(
    causal,
    q_ref,
    ko_ref,
    kx_ref,
    vo_ref,
    vx_ref,
    o_ref,
    do_ref,
    lse_ref,
    qi_ref,
    ki_ref,
    dq_ref,
    dko_ref,
    dkx_ref,
    dvo_ref,
    dvx_ref,
):
    length = q_ref.shape[1]
    heads = q_ref.shape[2] // HEAD
    block = length // 2
    segq = qi_ref[0:1, :]
    posq = qi_ref[1:2, :]
    ones = jnp.ones((8, HEAD), F32)
    for h in range(heads):
        cols = slice(h * HEAD, (h + 1) * HEAD)
        q_all = q_ref[0, :, cols] * jnp.asarray(SCALE, BF16)
        do_all = do_ref[0, :, cols]
        prod = do_all.astype(F32) * o_ref[0, :, cols].astype(F32)
        delta = dot_nt(ones, prod, precision=lax.Precision.HIGHEST)[0:1]
        lse = lse_ref[0, h : h + 1, :]
        dq = [jnp.zeros((block, HEAD), F32), jnp.zeros((block, HEAD), F32)]
        for k_ref, v_ref, dk_ref, dv_ref, i in (
            (ko_ref, vo_ref, dko_ref, dvo_ref, 0),
            (kx_ref, vx_ref, dkx_ref, dvx_ref, 2),
        ):
            for b in range(2):
                rows = slice(b * block, (b + 1) * block)
                first = b * block if causal else 0
                q = q_all[first:]
                do = do_all[first:]
                k = k_ref[0, rows, cols]
                s = dot_nt(k, q)
                ok = ki_ref[rows, i : i + 1] == segq[:, first:]
                if causal:
                    ok = ok & (posq[:, first:] >= ki_ref[rows, i + 1 : i + 2])
                p = jnp.where(ok, jnp.exp(s - lse[:, first:]), 0.0)
                dp = dot_nt(v_ref[0, rows, cols], do)
                ds = (p * (dp - delta[:, first:])).astype(BF16)
                dv_ref[0, rows, cols] = dot_nn(p.astype(BF16), do).astype(BF16)
                dk_ref[0, rows, cols] = dot_nn(ds, q).astype(BF16)
                part = dot_tn(ds, k)
                if first:
                    dq[1] = dq[1] + part
                else:
                    dq[0] = dq[0] + part[:block]
                    dq[1] = dq[1] + part[block:]
        dq_ref[0, :block, cols] = (dq[0] * SCALE).astype(BF16)
        dq_ref[0, block:, cols] = (dq[1] * SCALE).astype(BF16)


def attention_backward(q, k_own, k_oth, v_own, v_oth, o, do, lse, qi, ki, causal):
    groups, length, width = q.shape
    heads = width // HEAD
    spec = pl.BlockSpec((1, length, width), lambda t: (t, 0, 0))
    return pl.pallas_call(
        functools.partial(attn_bwd_kernel, causal),
        grid=(groups,),
        in_specs=[spec] * 7
        + [
            pl.BlockSpec((1, heads, length), lambda t: (t, 0, 0)),
            pl.BlockSpec(qi.shape, lambda t: (0, 0)),
            pl.BlockSpec(ki.shape, lambda t: (0, 0)),
        ],
        out_specs=[spec] * 5,
        out_shape=[jax.ShapeDtypeStruct(q.shape, BF16)] * 5,
        compiler_params=pltpu.CompilerParams(vmem_limit_bytes=48 * 2**20),
        name="attn_bwd",
    )(q, k_own, k_oth, v_own, v_oth, o, do, lse, qi, ki)


def norm(value):
    mean = jnp.mean(value, axis=-1, keepdims=True)
    centered = value - mean
    rstd = lax.rsqrt(jnp.mean(centered * centered, axis=-1, keepdims=True) + EPS)
    return centered * rstd, rstd


def norm_back(normed, rstd, grad):
    return rstd * (
        grad
        - jnp.mean(grad, axis=-1, keepdims=True)
        - normed * jnp.mean(grad * normed, axis=-1, keepdims=True)
    )


def project(rows, weight):
    return jnp.einsum("pk,tkm->tpm", rows, weight, preferred_element_type=F32)


def unproject(blocks, weight):
    return jnp.einsum("tpm,tkm->pk", blocks, weight, preferred_element_type=F32)


def self_forward(rows_bf, rows, w_attn, ids, causal):
    kv = [project(rows_bf, w_attn[:, j]).astype(BF16) for j in (1, 2)]
    other = swap(jnp.stack(kv))
    q = project(rows_bf, w_attn[:, 0]).astype(BF16)
    keys = (kv[0], other[0], kv[1], other[1])
    o, lse = attention_forward(q, *keys, *ids[0], causal)
    h, rstd = norm(rows + unproject(o, w_attn[:, 3]))
    return h, (q, keys, o, lse, h, rstd)


def attend_back(q, keys, o, do, lse, ids, causal):
    dq, dko, dkx, dvo, dvx = attention_backward(q, *keys, o, do, lse, *ids[1], causal)
    other = swap(jnp.stack([dkx, dvx])).astype(F32)
    dk = (dko.astype(F32) + other[0]).astype(BF16)
    dv = (dvo.astype(F32) + other[1]).astype(BF16)
    return dq, dk, dv


def self_backward(grad, kept, w_attn, ids, causal):
    q, keys, o, lse, h, rstd = kept
    dpre = norm_back(h, rstd, grad)
    do = project(dpre.astype(BF16), w_attn[:, 3]).astype(BF16)
    dq, dk, dv = attend_back(q, keys, o, do, lse, ids, causal)
    return (
        unproject(dq, w_attn[:, 0])
        + unproject(dk, w_attn[:, 1])
        + unproject(dv, w_attn[:, 2])
        + dpre
    )


def tail_forward(h, tail_w):
    w_in, w_out, a_in, b_in, a_out, b_out = tail_w
    rows = h.astype(BF16)
    inner = project(rows, w_in)
    phi = 0.5 * (1.0 + lax.erf(inner * 0.7071067811865476))
    g = (inner * phi).astype(BF16)
    slope = phi + inner * jnp.exp(inner * inner * -0.5) * 0.3989422804014327
    pre = project(rows, a_in) + b_in.astype(F32)[:, None, :]
    sig = jax.nn.sigmoid(pre)
    s = (pre * sig).astype(BF16)
    a_slope = sig * (1.0 + pre * (1.0 - sig))
    total = jnp.einsum("tpm,tmk->pk", g, w_out, preferred_element_type=F32)
    total += 4.0 * (
        jnp.einsum("tpm,tmk->pk", s, a_out, preferred_element_type=F32)
        + b_out.astype(F32)
    )
    y, rstd = norm(h + total)
    return y, (rows, slope.astype(BF16), s, a_slope.astype(BF16), y, rstd)


def tail_backward(grad, kept, tail_w):
    w_in, w_out, a_in, b_in, a_out, b_out = tail_w
    rows, slope, s, a_slope, y, rstd = kept
    dpre = norm_back(y, rstd, grad)
    db = dpre.astype(BF16)
    dg = jnp.einsum("pk,tmk->tpm", db, w_out, preferred_element_type=F32)
    df = (dg * slope.astype(F32)).astype(BF16)
    ds = 4.0 * jnp.einsum("pk,tmk->tpm", db, a_out, preferred_element_type=F32)
    du = (ds * a_slope.astype(F32)).astype(BF16)
    terms = (
        jnp.einsum("pk,tpm->tkm", rows, du, preferred_element_type=F32),
        jnp.sum(du.astype(F32), axis=1),
        4.0 * jnp.einsum("tpm,pk->tmk", s, db, preferred_element_type=F32),
        4.0 * jnp.sum(db.astype(F32), axis=0),
    )
    return unproject(df, w_in) + unproject(du, a_in) + dpre, terms


def gather_weights(shards):
    def one(shard):
        return lax.all_gather(lax.all_gather(shard, "tp"), "section")

    return [one(shard) for shard in shards]


def spread(blocks):
    chips = lax.axis_size("ctx") * lax.axis_size("tp")
    kinds, rows, part, width = blocks.shape
    blocks = jnp.pad(blocks, ((0, 0), (0, chips - rows), (0, 0), (0, 0)))
    moved = lax.all_to_all(
        jnp.moveaxis(blocks, 1, 0), ("ctx", "tp"), 0, 0, tiled=True
    )
    return jnp.moveaxis(moved, 0, 1).reshape(kinds, chips * part, width)


def collect(tokens, rows):
    chips = lax.axis_size("ctx") * lax.axis_size("tp")
    kinds, length, width = tokens.shape
    part = length // chips
    blocks = jnp.moveaxis(tokens.reshape(kinds, chips, part, width), 1, 0)
    moved = lax.all_to_all(blocks, ("ctx", "tp"), 0, 0, tiled=True)
    return jnp.moveaxis(moved, 0, 1)[:, :rows]


def per_device(
    layer_inputs,
    out_grad,
    src_seg,
    tgt_seg,
    qkv_weights,
    out_weights,
    cross_weights,
    ffn_in,
    ffn_out,
    adapter_in,
    adapter_in_bias,
    adapter_out,
    adapter_out_bias,
):
    core = lax.axis_index("section")
    is_first = core == 0
    tp = lax.axis_size("tp")
    chips = lax.axis_size("ctx") * tp
    chip = lax.axis_index("ctx") * tp + lax.axis_index("tp")
    _, micro, per_micro, part, width = layer_inputs.shape
    row_count = micro * per_micro
    half = part // 2
    length = half * chips

    def pick(first, second):
        return jnp.where(is_first, first, second)

    x = layer_inputs.reshape(row_count, part, width)
    low, high = x[:, :half], x[:, half:]
    other = swap(pick(high, low))
    grads = out_grad.reshape(row_count, part, width)
    stacked = jnp.stack(
        [pick(low, other), pick(other, high), pick(grads[:, :half], grads[:, half:])]
    )
    source, target, cotangent = spread(stacked)

    def ids_of(segments):
        flat = lax.all_gather(
            segments.reshape(row_count, -1), "ctx", axis=1, tiled=True
        )
        row = lax.dynamic_index_in_dim(
            flat, jnp.minimum(chip, row_count - 1), 0, keepdims=False
        )
        return row.reshape(chips, 2, half)

    index = jnp.arange(length, dtype=jnp.int32)
    place = (index // half) * part + index % half

    def cut(seg, which):
        own = lax.dynamic_index_in_dim(seg, which, 1, keepdims=False).reshape(length)
        return own, place + which * half

    src_ids, tgt_ids = ids_of(src_seg), ids_of(tgt_seg)

    def id_arrays(seg_q, seg_k):
        qi = jnp.stack(cut(seg_q, core))
        ki = jnp.stack(cut(seg_k, core) + cut(seg_k, 1 - core))
        return (qi.T, ki), (qi, ki.T)

    enc_ids = id_arrays(src_ids, src_ids)
    dec_ids = id_arrays(tgt_ids, tgt_ids)
    cross_ids = id_arrays(tgt_ids, src_ids)

    w_attn, w_cross, w_in, w_out, a_in, b_in, a_out = gather_weights(
        [
            jnp.concatenate([qkv_weights[0], out_weights], axis=0),
            cross_weights[0],
            ffn_in[0],
            ffn_out[0],
            adapter_in[0],
            adapter_in_bias[0],
            adapter_out[0],
        ]
    )
    b_out = lax.all_gather(adapter_out_bias[0], "section")
    tails = [
        (w_in[e], w_out[e], a_in[e], b_in[e], a_out[e], b_out[e]) for e in range(2)
    ]

    enc_mid, enc_self = self_forward(
        source, source.astype(F32), w_attn[0], enc_ids, False
    )
    encoded, enc_tail = tail_forward(enc_mid, tails[0])
    encoded_bf = encoded.astype(BF16)
    memory = [project(encoded_bf, w_cross[0, :, j]).astype(BF16) for j in range(2)]
    memory_other = swap(jnp.stack(memory))
    mem_keys = (memory[0], memory_other[0], memory[1], memory_other[1])

    dec_mid, dec_self = self_forward(
        target, target.astype(F32), w_attn[1], dec_ids, True
    )
    queries = project(dec_mid.astype(BF16), w_cross[1, :, 0]).astype(BF16)
    cross_o, cross_lse = attention_forward(
        queries, *mem_keys, *cross_ids[0], False
    )
    second, second_rstd = norm(dec_mid + unproject(cross_o, w_cross[1, :, 1]))
    decoded, dec_tail = tail_forward(second, tails[1])

    grad_second, dec_terms = tail_backward(cotangent.astype(F32), dec_tail, tails[1])
    grad_cross = norm_back(second, second_rstd, grad_second)
    do = project(grad_cross.astype(BF16), w_cross[1, :, 1]).astype(BF16)
    dqc, dmk, dmv = attend_back(
        queries, mem_keys, cross_o, do, cross_lse, cross_ids, False
    )
    grad_first = unproject(dqc, w_cross[1, :, 0]) + grad_cross
    grad_target = self_backward(grad_first, dec_self, w_attn[1], dec_ids, True)

    grad_encoded = unproject(dmk, w_cross[0, :, 0]) + unproject(dmv, w_cross[0, :, 1])
    grad_mid, enc_terms = tail_backward(grad_encoded, enc_tail, tails[0])
    grad_source = self_backward(grad_mid, enc_self, w_attn[0], enc_ids, False)

    has_row = chip < row_count

    def total(enc_term, dec_term):
        enc_term = jnp.where(has_row, enc_term, 0.0).astype(BF16)
        dec_term = jnp.where(has_row, dec_term, 0.0).astype(BF16)
        got = swap(pick(dec_term, enc_term))
        return (pick(enc_term, dec_term).astype(F32) + got.astype(F32)).astype(BF16)

    sums = [total(e, d) for e, d in zip(enc_terms, dec_terms)]
    scattered = [
        lax.psum_scatter(v, "tp", scatter_dimension=0, tiled=False) for v in sums[:3]
    ]
    scattered = [lax.psum(v, "ctx").astype(F32) for v in scattered]
    bias_sum = lax.psum(sums[3], ("ctx", "tp")).astype(F32)

    results = jnp.stack(
        [
            encoded_bf,
            decoded.astype(BF16),
            grad_source.astype(BF16),
            grad_target.astype(BF16),
        ]
    )
    placed = collect(results, row_count)

    def join(enc_part, dec_part):
        mine = pick(enc_part, dec_part)
        got = swap(pick(dec_part, enc_part))
        return jnp.concatenate([pick(mine, got), pick(got, mine)], axis=1)

    outs = join(placed[0], placed[1]).reshape(layer_inputs.shape)
    grads = join(placed[2], placed[3]).astype(F32).reshape(layer_inputs.shape)
    return (
        outs,
        grads,
        scattered[0][None],
        scattered[1][None],
        scattered[2][None],
        bias_sum[None],
    )


def solution(mesh):
    return jax.shard_map(
        per_device,
        mesh=mesh,
        in_specs=(
            P("section", None, None, ("ctx", "tp"), None),
            P(None, None, ("ctx", "tp"), None),
            P(None, None, "ctx"),
            P(None, None, "ctx"),
            P("section", None, None, "tp"),
            P("section", None, "tp"),
            P("section", None, None, "tp"),
            P("section", None, "tp"),
            P("section", "tp", None),
            P("section", None, "tp"),
            P("section", "tp"),
            P("section", "tp", None),
            P("section", None),
        ),
        out_specs=(
            P("section", None, None, ("ctx", "tp"), None),
            P("section", None, None, ("ctx", "tp"), None),
            P("section", None, "tp"),
            P("section", "tp"),
            P("section", "tp", None),
            P("section", None),
        ),
        check_vma=False,
    )
```

time: 5720 us -> 1310 us (0.23)
  waiting for transfers between devices: 3950 us -> 759 us
  matrix products: 1050 us -> 174 us
  other arithmetic: 396 us -> 45.6 us
  Pallas kernels: 0 us -> 153 us
  local copies, waits for them, and re-layouts: 155 us -> 43.6 us
    reduce_scatter x102 -> x2, waiting for transfers between devices: 2410 us -> 0.01 us  [per_device(): lax.psum_scatter(v, 'tp', scatter_dimension=0, tiled=False)]
    dot_general x288 -> x42, matrix products: 1050 us -> 174 us  [the longest x16 73.4 us: project(): return jnp.einsum('pk,tkm->tpm', rows, weight, preferred_element_type=F32)]
    all_gather x84 -> x12, waiting for transfers between devices: 1480 us -> 631 us  [one(): return lax.all_gather(lax.all_gather(shard, 'tp'), 'section')]
    reduce_sum x106 -> x8, other arithmetic: 174 us -> 8.45 us  [the longest x2 5.18 us: tail_backward(): jnp.sum(db.astype(F32), axis=0)]
    pallas_call x0 -> x6, Pallas kernels: none -> 153 us  [the longest x3 89.4 us: attention_backward(): pl.pallas_call(functools.partial(attn_bwd_kernel, causal), grid=(groups,)...]
    convert_element_type x51 -> x13, other arithmetic: 139 us -> 15.4 us  [the longest x3 4.95 us: attend_back(): other = swap(jnp.stack([dkx, dvx])).astype(F32)]
    all_to_all x0 -> x2, waiting for transfers between devices: none -> 118 us  [the longest x1 118 us: collect(): moved = lax.all_to_all(blocks, ('ctx', 'tp'), 0, 0, tiled=True)]
    unnamed x1420 -> x190, local copies, waits for them, and re-layouts: 76.4 us -> 15.6 us
  transfers between devices with their start and end apart: 194 -> 30, of which waited for: 179 -> 14; matrix products, arithmetic and copies ran while one was open for 22% -> 13% of each run, Pallas kernels for 0% -> 8%
where the time goes in v1:
time: 1310 us; the launch traced here: 1300 us
  waiting for transfers between devices  759 us (58%)
  matrix products  174 us (13%)
  Pallas kernels  153 us (12%)
  blocking collectives  94.7 us (7%)
  other arithmetic  45.6 us (3%)
  local copies, waits for them, and re-layouts  43.6 us (3%)
  between operations  15.8 us (1%)
  starting transfers between devices  15.5 us (1%)
    all_gather x12, waiting for transfers between devices, one(): return lax.all_gather(lax.all_gather(shard, 'tp'), 'section')  631 us
    all_to_all x1, waiting for transfers between devices, collect(): moved = lax.all_to_all(blocks, ('ctx', 'tp'), 0, 0, tiled=True)  118 us
    pallas_call x3, Pallas kernels, attention_backward(): pl.pallas_call(functools.partial(attn_bwd_kernel, causal), grid=(groups,)...  89.4 us
    dot_general x16, matrix products, project(): return jnp.einsum('pk,tkm->tpm', rows, weight, preferred_element_type=F32)  73.4 us
    dot_general x16, matrix products, unproject(): return jnp.einsum('tpm,tkm->pk', blocks, weight, preferred_element_type=F32)  68 us
    pallas_call x3, Pallas kernels, attention_forward(): pl.pallas_call(functools.partial(attn_fwd_kernel, causal), grid=(groups,)...  63.4 us
    psum x1, blocking collectives, per_device(): bias_sum = lax.psum(sums[3], ('ctx', 'tp')).astype(F32)  40.4 us
  transfers between devices with their start and end apart: 30, of which 14 were waited for; matrix products, arithmetic and copies ran while one was open for 13% of the time, Pallas kernels for 8%

profile of v1, /device:TPU:0, one launch (start us, length us, event | category | flops | bytes accessed | tf_op | source)
XLA Modules:
  0.0 1301.6 jit_solution(15631305149514327971)
XLA Ops:
  13.6 149.2 %all-gather.34.cloned.1.call-done = bf16[16,1024,256]{2,1,0:T(8,128)(2,1)} async-done(((bf16[4,1024,256]{2,1,0:T(8,128)(2,1)}), bf16[16,1024,256]{2,1,0:T(8,128)(2,1)}) %all-gather.34.cloned.1.call-update) | async-done | bytes 8388624 | tf_op jit(solution)/shard_map/all_gather | solution.py:274
  162.8 11.5 copy.86
  174.4 16.1 %all-gather.28.cloned.1.call-done = bf16[4,1024,128]{2,1,0:T(8,128)(2,1)} async-done(((bf16[1,1024,128]{2,1,0:T(8,128)(2,1)}), bf16[4,1024,128]{2,1,0:T(8,128)(2,1)}) %all-gather.28.cloned.1.call-update) | async-done | bytes 1048592 | tf_op jit(solution)/shard_map/all_gather | solution.py:274
  190.6 150.7 %all-gather.24.cloned.1.call-done = bf16[4,1024,1024]{2,1,0:T(8,128)(2,1)} async-done(((bf16[1,1024,1024]{2,1,0:T(8,128)(2,1)}), bf16[4,1024,1024]{2,1,0:T(8,128)(2,1)}) %all-gather.24.cloned.1.call-update) | async-done | bytes 8388624 | tf_op jit(solution)/shard_map/all_gather | solution.py:274
  341.4 149.3 %all-gather.26.cloned.1.call-done = bf16[4,1024,1024]{2,1,0:T(8,128)(2,1)} async-done(((bf16[1,1024,1024]{2,1,0:T(8,128)(2,1)}), bf16[4,1024,1024]{2,1,0:T(8,128)(2,1)}) %all-gather.26.cloned.1.call-update) | async-done | bytes 8388624 | tf_op jit(solution)/shard_map/all_gather | solution.py:274
  501.2 45.5 %all-gather.30.cloned.1.call-done = bf16[4,128,1024]{2,1,0:T(8,128)(2,1)} async-done(((bf16[1,128,1024]{2,1,0:T(8,128)(2,1)}), bf16[4,128,1024]{2,1,0:T(8,128)(2,1)}) %all-gather.30.cloned.1.call-update) | async-done | bytes 1048592 | tf_op jit(solution)/shard_map/all_gather | solution.py:274
  546.8 10.5 all_gather.79
  557.4 7.5 all_gather.96
  566.4 16.2 %all-gather.8 = bf16[4,1,128]{2,1,0:T(2,128)(2,1)S(1)} all-gather(bf16[1,1,128]{2,1,0:T(2,128)(2,1)S(1)} %bitcast.595), channel_id=1, replica_groups=mesh['section'=2,'ctx'=4,'tp'=4] {'tp'}, dimensions={0}, use_global_device_ids=true | all-gather | bytes 1280 | tf_op jit(solution)/shard_map/all_gather | solution.py:274
  587.7 66.0 %all-gather.32.cloned.1.call-done = bf16[4,2,1024,256]{3,2,1,0:T(8,128)(2,1)} async-done(((bf16[1,2,1024,256]{3,2,1,0:T(8,128)(2,1)}), bf16[4,2,1024,256]{3,2,1,0:T(8,128)(2,1)}) %all-gather.32.cloned.1.call-update) | async-done | bytes 4194320 | tf_op jit(solution)/shard_map/all_gather | solution.py:274
  656.5 27.7 %all-gather.36.cloned.1.call-done = bf16[8,4,1024,256]{2,3,0,1:T(8,128)(2,1)} async-done(((bf16[4,4,1024,256]{2,3,0,1:T(8,128)(2,1)}), bf16[8,4,1024,256]{2,3,0,1:T(8,128)(2,1)}) %all-gather.36.cloned.1.call-update) | async-done | bytes 16777232 | tf_op jit(solution)/shard_map/all_gather | solution.py:274
  710.6 21.0 %attn_fwd.3 = (bf16[4,512,256]{2,1,0:T(8,128)(2,1)S(1)}, f32[4,4,512]{2,1,0:T(4,128)S(1)}) custom-call(bf16[4,512,256]{2,1,0:T(8,128)(2,1)S(1)} %fusion.124.q_ref, bf16[4,512,256]{2,1,0:T(8,128)(2,1)S(1)} %bitcast.530, bf16[4,512,256]{2,1,0:T(8,128)(2,1)S(1)} %get-tuple-element.103.kx_ref, bf16[4,512,256]{2,1,0:T(8,128)(2,1)S(1)} %bitcast.533, ...), custom_call_target="tpu_custom_call" | custom-call | tf_op jit(solution)/shard_map/attn_fwd/pallas_call | solution.py:81
  739.9 16.0 %fusion.32 = f32[512,4,1024]{2,0,1:T(8,128)} fusion(bf16[512,1024,1]{1,0,2:T(8,128)(2,1)} %fusion.144, bf16[8,1024,1024]{2,1,0:T(8,128)(2,1)} %all-gather.38.cloned.1.call-done), kind=kOutput, calls=%fused_computation.42 | convolution fusion | flops 4294967296 | bytes 17825792 | tf_op jit(solution)/shard_map/pk,tkm->tpm/dot_general | solution.py:196
  755.9 7.4 all-gather.40.cloned.1.call-done
  763.3 11.6 fusion.28
  781.5 17.6 %all-gather.46.cloned.1.call-done = bf16[8,2,1024,256]{3,2,1,0:T(8,128)(2,1)} async-done(((bf16[4,2,1024,256]{3,2,1,0:T(8,128)(2,1)}), bf16[8,2,1024,256]{3,2,1,0:T(8,128)(2,1)}) %all-gather.46.cloned.1.call-update) | async-done | bytes 8388624 | tf_op jit(solution)/shard_map/all_gather | solution.py:274
  813.1 21.2 %attn_fwd.4 = (bf16[4,512,256]{2,1,0:T(8,128)(2,1)S(1)}, f32[4,4,512]{2,1,0:T(4,128)S(1)}) custom-call(bf16[4,512,256]{2,1,0:T(8,128)(2,1)S(1)} %fusion.126.q_ref, bf16[4,512,256]{2,1,0:T(8,128)(2,1)S(1)} %bitcast.540, bf16[4,512,256]{2,1,0:T(8,128)(2,1)S(1)} %get-tuple-element.105.kx_ref, bf16[4,512,256]{2,1,0:T(8,128)(2,1)S(1)} %bitcast.536, ...), custom_call_target="tpu_custom_call" | custom-call | tf_op jit(solution)/shard_map/attn_fwd/pallas_call | solution.py:81
  842.6 21.2 %attn_fwd.5 = (bf16[4,512,256]{2,1,0:T(8,128)(2,1)S(1)}, f32[4,4,512]{2,1,0:T(4,128)S(1)}) custom-call(bf16[4,512,256]{2,1,0:T(8,128)(2,1)S(1)} %fusion.128.q_ref, bf16[4,512,256]{2,1,0:T(8,128)(2,1)S(1)} %bitcast.545, bf16[4,512,256]{2,1,0:T(8,128)(2,1)S(1)} %get-tuple-element.101.kx_ref, bf16[4,512,256]{2,1,0:T(8,128)(2,1)S(1)} %bitcast.542, ...), custom_call_target="tpu_custom_call" | custom-call | tf_op jit(solution)/shard_map/attn_fwd/pallas_call | solution.py:81
  867.9 11.2 fusion.24
  879.2 8.0 fusion.20
  897.1 14.4 %fusion.26 = f32[512,1024,1]{1,0,2:T(8,128)} fusion(bf16[8,1024,1024]{2,1,0:T(8,128)(2,1)} %all-gather.38.cloned.1.call-done, f32[512,4,1024]{2,0,1:T(8,128)} %fusion.24, bf16[8,1024,1024]{2,1,0:T(8,128)(2,1)} %all-gather.40.cloned.1.call-done, bf16[512,1024]{1,0:T(8,128)(2,1)S(1)} %get-tuple-element.81), kind=kOutput, calls=%fused_computation.36 | convolution fusion | flops 8615100416 | bytes 28311552 | tf_op jit(solution)/shard_map/tpm,tkm->pk/dot_general | solution.py:200
  916.6 4.8 fusion.129.do_ref
  921.4 31.2 %attn_bwd.3 = (bf16[4,512,256]{2,1,0:T(8,128)(2,1)S(1)}, bf16[4,512,256]{2,1,0:T(8,128)(2,1)S(1)}, bf16[4,512,256]{2,1,0:T(8,128)(2,1)S(1)}, bf16[4,512,256]{2,1,0:T(8,128)(2,1)S(1)}, bf16[4,512,256]{2,1,0:T(8,128)(2,1)S(1)}) custom-call(bf16[4,512,256]{2,1,0:T(8,128)(2,1)} %copy-done.12, bf16[4,512,256]{2,1,0:T(8,128)(2,1)} %bitcast.546, ...), custom_call_target="tpu_custom_call" | custom-call | tf_op jit(solution)/shard_map/attn_bwd/pallas_call | solution.py:164
  964.1 27.1 %attn_bwd.5 = (bf16[4,512,256]{2,1,0:T(8,128)(2,1)S(1)}, bf16[4,512,256]{2,1,0:T(8,128)(2,1)S(1)}, bf16[4,512,256]{2,1,0:T(8,128)(2,1)S(1)}, bf16[4,512,256]{2,1,0:T(8,128)(2,1)S(1)}, bf16[4,512,256]{2,1,0:T(8,128)(2,1)S(1)}) custom-call(bf16[4,512,256]{2,1,0:T(8,128)(2,1)} %copy-done.11, bf16[4,512,256]{2,1,0:T(8,128)(2,1)} %bitcast.539, ...), custom_call_target="tpu_custom_call" | custom-call | tf_op jit(solution)/shard_map/attn_bwd/pallas_call | solution.py:164
  1001.5 14.9 %fusion.34 = f32[512,1024,1]{1,0,2:T(8,128)} fusion(bf16[8,1024,1024]{2,1,0:T(8,128)(2,1)} %all-gather.38.cloned.1.call-done, f32[512,4,1024]{2,0,1:T(8,128)} %fusion.32, bf16[8,1024,1024]{2,1,0:T(8,128)(2,1)} %all-gather.40.cloned.1.call-done, bf16[512,1024]{1,0:T(8,128)(2,1)S(1)} %get-tuple-element.84), kind=kOutput, calls=%fused_computation.44 | convolution fusion | flops 8615100416 | bytes 28311552 | tf_op jit(solution)/shard_map/tpm,tkm->pk/dot_general | solution.py:200
  1021.6 4.9 fusion.125.do_ref
  1026.5 31.1 %attn_bwd.4 = (bf16[4,512,256]{2,1,0:T(8,128)(2,1)S(1)}, bf16[4,512,256]{2,1,0:T(8,128)(2,1)S(1)}, bf16[4,512,256]{2,1,0:T(8,128)(2,1)S(1)}, bf16[4,512,256]{2,1,0:T(8,128)(2,1)S(1)}, bf16[4,512,256]{2,1,0:T(8,128)(2,1)S(1)}) custom-call(bf16[4,512,256]{2,1,0:T(8,128)(2,1)} %copy-done.10, bf16[4,512,256]{2,1,0:T(8,128)(2,1)} %bitcast.531, ...), custom_call_target="tpu_custom_call" | custom-call | tf_op jit(solution)/shard_map/attn_bwd/pallas_call | solution.py:164
  1082.6 7.1 all-to-all-start.1
  1104.0 117.8 %all-to-all-done.1 = bf16[16,4,32,1024]{3,2,1,0:T(8,128)(2,1)} async-done(((bf16[16,4,32,1024]{3,2,1,0:T(8,128)(2,1)}), bf16[16,4,32,1024]{3,2,1,0:T(8,128)(2,1)}, u32[]{:S(2)}, u32[]{:S(2)}) %all-to-all-start.1) | async-done | bytes 4194336 | tf_op jit(solution)/shard_map/all_to_all | solution.py:294
  1227.3 8.4 all-reduce.1
  1236.4 7.6 psum.29
  1244.5 40.4 %psum.31 = bf16[1,1024]{1,0:T(2,128)(2,1)S(1)} all-reduce(bf16[1,1024]{1,0:T(2,128)(2,1)S(1)} %broadcast_in_dim.75), channel_id=1, replica_groups=mesh['section'=2,'ctx'=4,'tp'=4] {'ctx','tp'}, use_global_device_ids=true, to_apply=%region_30.31 | all-reduce | flops 1024 | bytes 4096 | tf_op jit(solution)/shard_map/psum | solution.py:423
  (381 shorter events, 190.7 us)
Async XLA Ops:
  7.2 155.6 %all-gather.34.cloned.1.call-start = ((), (), s32[]{:S(2)}) async-start(), calls=%async_computation.11 | async-start | bytes 10485760 | tf_op jit(solution)/shard_map/all_gather | solution.py:274
  10.3 180.2 %all-gather.28.cloned.1.call-start = ((), (), s32[]{:S(2)}) async-start(), calls=%async_computation.6 | async-start | bytes 1310720 | tf_op jit(solution)/shard_map/all_gather | solution.py:274
  11.1 330.2 %all-gather.24.cloned.1.call-start = ((), (), s32[]{:S(2)}) async-start(), calls=%async_computation.4 | async-start | bytes 10485760 | tf_op jit(solution)/shard_map/all_gather | solution.py:274
  11.8 478.8 %all-gather.26.cloned.1.call-start = ((), (), s32[]{:S(2)}) async-start(), calls=%async_computation.5 | async-start | bytes 10485760 | tf_op jit(solution)/shard_map/all_gather | solution.py:274
  12.4 534.3 %all-gather.30.cloned.1.call-start = ((), (), s32[]{:S(2)}) async-start(), calls=%async_computation.7 | async-start | bytes 1310720 | tf_op jit(solution)/shard_map/all_gather | solution.py:274
  13.0 640.7 %all-gather.32.cloned.1.call-start = ((), (), s32[]{:S(2)}) async-start(), calls=%async_computation.8 | async-start | bytes 5242880 | tf_op jit(solution)/shard_map/all_gather | solution.py:274
  13.5 670.6 %all-gather.36.cloned.1.call-start = ((), (), s32[]{:S(2)}) async-start(), calls=%async_computation.12 | async-start | bytes 25165824 | tf_op jit(solution)/shard_map/all_gather | solution.py:274
  174.4 562.3 %all-gather.42.cloned.1.call-start = ((), (), s32[]{:S(2)}) async-start(), calls=%async_computation.15 | async-start | bytes 3145728 | tf_op jit(solution)/shard_map/all_gather | solution.py:274
  190.6 549.3 %all-gather.38.cloned.1.call-start = ((), (), s32[]{:S(2)}) async-start(), calls=%async_computation.13 | async-start | bytes 25165824 | tf_op jit(solution)/shard_map/all_gather | solution.py:274
  341.3 422.0 %all-gather.40.cloned.1.call-start = ((), (), s32[]{:S(2)}) async-start(), calls=%async_computation.14 | async-start | bytes 25165824 | tf_op jit(solution)/shard_map/all_gather | solution.py:274
  492.1 2.4 collective-permute-start
  496.5 157.2 %all-to-all-start = ((bf16[16,3,32,1024]{3,2,1,0:T(8,128)(2,1)}), bf16[16,3,32,1024]{3,2,1,0:T(8,128)(2,1)}, u32[]{:S(2)}, u32[]{:S(2)}) async-start(bf16[16,3,32,1024]{3,2,1,0:T(8,128)(2,1)} %fusion.57), calls=%async_computation | async-start | bytes 6291456 | tf_op jit(solution)/shard_map/all_to_all | solution.py:283
  501.2 275.5 %all-gather.44.cloned.1.call-start = ((), (), s32[]{:S(2)}) async-start(), calls=%async_computation.16 | async-start | bytes 3145728 | tf_op jit(solution)/shard_map/all_gather | solution.py:274
  546.7 252.4 %all-gather.46.cloned.1.call-start = ((), (), s32[]{:S(2)}) async-start(), calls=%async_computation.17 | async-start | bytes 12582912 | tf_op jit(solution)/shard_map/all_gather | solution.py:274
  565.5 88.2 %copy-start.18 = (s32[2,512]{1,0:T(2,128)}, s32[2,512]{1,0:T(2,128)S(1)}, u32[]{:S(2)}) copy-start(s32[2,512]{1,0:T(2,128)S(1)} %get-tuple-element.112.qi_ref) | copy-start | bytes 12292
  692.0 15.1 %collective-permute-start.1 = (bf16[2,4,512,256]{3,2,1,0:T(8,128)(2,1)}, bf16[2,4,512,256]{3,2,1,0:T(8,128)(2,1)}, u32[]{:S(2)}, u32[]{:S(2)}) collective-permute-start(bf16[2,4,512,256]{3,2,1,0:T(8,128)(2,1)} %pad_maximum_fusion.1), channel_id=1, source_target_pairs={{0,16},{16,0},{1,17},{17,1},{2,18},{18,2},{3,19},{19,3},{4,20},{20... | collective-permute-start | bytes 6291464 | tf_op jit(solution)/shard_map/ppermute | solution.py:19
  698.9 114.2 %copy-start.3 = (bf16[4,256,512]{1,2,0:T(8,128)(2,1)}, bf16[4,256,512]{1,2,0:T(8,128)(2,1)S(1)}, u32[]{:S(2)}) copy-start(bf16[4,256,512]{1,2,0:T(8,128)(2,1)S(1)} %fusion.117) | copy-start | bytes 3145732
  703.9 106.1 %collective-permute-start.2 = (bf16[2,4,512,256]{3,2,1,0:T(8,128)(2,1)}, bf16[2,4,512,256]{3,2,1,0:T(8,128)(2,1)}, u32[]{:S(2)}, u32[]{:S(2)}) collective-permute-start(bf16[2,4,512,256]{3,2,1,0:T(8,128)(2,1)} %pad_maximum_fusion.2), channel_id=1, source_target_pairs={{0,16},{16,0},{1,17},{17,1},{2,18},{18,2},{3,19},{19,3},{4,20},{20... | collective-permute-start | bytes 6291464 | tf_op jit(solution)/shard_map/ppermute | solution.py:19
  805.7 35.7 %collective-permute-start.3 = (bf16[2,4,512,256]{3,2,1,0:T(8,128)(2,1)S(1)}, bf16[2,4,512,256]{3,2,1,0:T(8,128)(2,1)S(1)}, u32[]{:S(2)}, u32[]{:S(2)}) collective-permute-start(bf16[2,4,512,256]{3,2,1,0:T(8,128)(2,1)S(1)} %pad_maximum_fusion.3), channel_id=1, source_target_pairs={{0,16},{16,0},{1,17},{17,1},{2,18},{18,2},{3,19},{19,3},{4,20},{20... | collective-permute-start | bytes 6291464 | tf_op jit(solution)/shard_map/ppermute | solution.py:19
  954.2 39.5 %collective-permute-start.4 = (bf16[2,4,512,256]{3,2,1,0:T(8,128)(2,1)}, bf16[2,4,512,256]{3,2,1,0:T(8,128)(2,1)}, u32[]{:S(2)}, u32[]{:S(2)}) collective-permute-start(bf16[2,4,512,256]{3,2,1,0:T(8,128)(2,1)} %pad_maximum_fusion.4), channel_id=1, source_target_pairs={{0,16},{16,0},{1,17},{17,1},{2,18},{18,2},{3,19},{19,3},{4,20},{20... | collective-permute-start | bytes 6291464 | tf_op jit(solution)/shard_map/ppermute | solution.py:19
  993.4 68.4 %collective-permute-start.6 = (bf16[2,4,512,256]{3,2,1,0:T(8,128)(2,1)}, bf16[2,4,512,256]{3,2,1,0:T(8,128)(2,1)}, u32[]{:S(2)}, u32[]{:S(2)}) collective-permute-start(bf16[2,4,512,256]{3,2,1,0:T(8,128)(2,1)} %pad_maximum_fusion.6), channel_id=1, source_target_pairs={{0,16},{16,0},{1,17},{17,1},{2,18},{18,2},{3,19},{19,3},{4,20},{20... | collective-permute-start | bytes 6291464 | tf_op jit(solution)/shard_map/ppermute | solution.py:19
  1057.9 15.3 %collective-permute-start.5 = (bf16[2,4,512,256]{3,2,1,0:T(8,128)(2,1)S(1)}, bf16[2,4,512,256]{3,2,1,0:T(8,128)(2,1)S(1)}, u32[]{:S(2)}, u32[]{:S(2)}) collective-permute-start(bf16[2,4,512,256]{3,2,1,0:T(8,128)(2,1)S(1)} %pad_maximum_fusion.5), channel_id=1, source_target_pairs={{0,16},{16,0},{1,17},{17,1},{2,18},{18,2},{3,19},{19,3},{4,20},{20... | collective-permute-start | bytes 6291464 | tf_op jit(solution)/shard_map/ppermute | solution.py:19
  1082.6 139.2 %all-to-all-start.1 = ((bf16[16,4,32,1024]{3,2,1,0:T(8,128)(2,1)}), bf16[16,4,32,1024]{3,2,1,0:T(8,128)(2,1)}, u32[]{:S(2)}, u32[]{:S(2)}) async-start(bf16[16,4,32,1024]{3,2,1,0:T(8,128)(2,1)} %maximum_bitcast_fusion), calls=%async_computation.1 | async-start | bytes 8388608 | tf_op jit(solution)/shard_map/all_to_all | solution.py:294
  1089.7 137.6 %reduce-scatter.5.cloned.1.call-start = ((), (), s32[]{:S(2)}) async-start(), calls=%async_computation.10 | async-start | bytes 1310720 | tf_op jit(solution)/shard_map/reduce_scatter | solution.py:420
  1092.1 2.7 collective-permute-start.11
  1096.5 130.8 %reduce-scatter.3.cloned.1.call-start = ((), (), s32[]{:S(2)}) async-start(), calls=%async_computation.9 | async-start | bytes 1310720 | tf_op jit(solution)/shard_map/reduce_scatter | solution.py:420
  1098.7 2.7 collective-permute-start.9
  1103.1 182.5 %all-reduce.5.cloned.1.call-start = ((), (), s32[]{:S(2)}) async-start(), calls=%async_computation.18 | async-start | bytes 1048576 | tf_op jit(solution)/shard_map/psum | solution.py:422
  1103.8 123.6 %collective-permute-start.10 = (bf16[4,128]{1,0:T(4,128)(2,1)S(1)}, bf16[4,128]{1,0:T(4,128)(2,1)S(1)}, u32[]{:S(2)}, u32[]{:S(2)}) collective-permute-start(bf16[4,128]{1,0:T(4,128)(2,1)S(1)} %broadcast_select_fusion.5), channel_id=1, source_target_pairs={{0,16},{16,0},{1,17},{17,1},{2,18},{18,2},{3,19},{19,3},{4,20},{20... | collective-permute-start | bytes 3080 | tf_op jit(solution)/shard_map/ppermute | solution.py:19
  1226.6 62.6 %collective-permute-start.7 = (bf16[12,32,1024]{2,1,0:T(8,128)(2,1)S(1)}, bf16[12,32,1024]{2,1,0:T(8,128)(2,1)S(1)}, u32[]{:S(2)}, u32[]{:S(2)}) collective-permute-start(bf16[12,32,1024]{2,1,0:T(8,128)(2,1)S(1)} %get-tuple-element.93), channel_id=1, source_target_pairs={{0,16},{16,0},{1,17},{17,1},{2,18},{18,2},{3,19},{19,3},{4,20},{20... | collective-permute-start | bytes 2359304 | tf_op jit(solution)/shard_map/ppermute | solution.py:19
  1226.7 62.5 %collective-permute-start.8 = (bf16[12,32,1024]{2,1,0:T(8,128)(2,1)S(1)}, bf16[12,32,1024]{2,1,0:T(8,128)(2,1)S(1)}, u32[]{:S(2)}, u32[]{:S(2)}) collective-permute-start(bf16[12,32,1024]{2,1,0:T(8,128)(2,1)S(1)} %get-tuple-element.92), channel_id=1, source_target_pairs={{0,16},{16,0},{1,17},{17,1},{2,18},{18,2},{3,19},{19,3},{4,20},{20... | collective-permute-start | bytes 2359304 | tf_op jit(solution)/shard_map/ppermute | solution.py:19
  1227.2 17.3 %collective-permute-start.12 = (bf16[1024]{0:T(1024)(128)(2,1)S(1)}, bf16[1024]{0:T(1024)(128)(2,1)S(1)}, u32[]{:S(2)}, u32[]{:S(2)}) collective-permute-start(bf16[1024]{0:T(1024)(128)(2,1)S(1)} %broadcast_select_fusion.4), channel_id=1, source_target_pairs={{0,16},{16,0},{1,17},{17,1},{2,18},{18,2},{3,19},{19,3},{4,20},{20... | collective-permute-start | bytes 6152 | tf_op jit(solution)/shard_map/ppermute | solution.py:19
  (91 other events, 973.8 us)
Sparse Core Ops, SparseCore 0:
  10.4 152.3 all-gather.33
  164.4 26.1 all-gather.27
  192.1 149.1 all-gather.23
  342.7 147.8 all-gather.25
  492.0 54.6 all-gather.29
  548.1 105.5 all-gather.31
  655.3 28.8 all-gather.35
  685.7 12.0 all-gather.41
  699.4 31.2 all-gather.37
  732.1 31.2 all-gather.39
  764.9 11.7 all-gather.43
  778.1 21.0 all-gather.45
  1096.6 68.1 reduce-scatter.4
  1167.6 37.1 reduce-scatter.2
  1227.4 42.1 all-reduce.4

commit v2 on v1

--- a/solution.py
+++ b/solution.py
@@ -244,7 +244,7 @@
     a_slope = sig * (1.0 + pre * (1.0 - sig))
     total = jnp.einsum("tpm,tmk->pk", g, w_out, preferred_element_type=F32)
     total += 4.0 * (
-        jnp.einsum("tpm,tmk->pk", s, a_out, preferred_element_type=F32)
+        jnp.einsum("tpm,tkm->pk", s, a_out, preferred_element_type=F32)
         + b_out.astype(F32)
     )
     y, rstd = norm(h + total)
@@ -258,7 +258,7 @@
     db = dpre.astype(BF16)
     dg = jnp.einsum("pk,tmk->tpm", db, w_out, preferred_element_type=F32)
     df = (dg * slope.astype(F32)).astype(BF16)
-    ds = 4.0 * jnp.einsum("pk,tmk->tpm", db, a_out, preferred_element_type=F32)
+    ds = 4.0 * jnp.einsum("pk,tkm->tpm", db, a_out, preferred_element_type=F32)
     du = (ds * a_slope.astype(F32)).astype(BF16)
     terms = (
         jnp.einsum("pk,tpm->tkm", rows, du, preferred_element_type=F32),
@@ -269,11 +269,270 @@
     return unproject(df, w_in) + unproject(du, a_in) + dpre, terms
 
 
-def gather_weights(shards):
-    def one(shard):
-        return lax.all_gather(lax.all_gather(shard, "tp"), "section")
-
-    return [one(shard) for shard in shards]
+def remote(src, dst, send, recv, where):
+    return pltpu.make_async_remote_copy(
+        src_ref=src,
+        dst_ref=dst,
+        send_sem=send,
+        recv_sem=recv,
+        device_id=where,
+        device_id_type=pl.DeviceIdType.MESH,
+    )
+
+
+def gather_kernel(entry, groups, window, *refs):
+    shards = refs[:groups]
+    tokens, = refs[groups : groups + 1]
+    outs = refs[groups + 1 : 2 * groups + 1]
+    placed = refs[2 * groups + 1]
+    (
+        z_send,
+        z_recv,
+        n_send,
+        n_recv,
+        f_send,
+        f_recv,
+        s_send,
+        s_recv,
+        own_sem,
+        t_send,
+        t_recv,
+    ) = refs[2 * groups + 2 : 2 * groups + 13]
+    stores = refs[2 * groups + 13 : 3 * groups + 13]
+    token_store = refs[3 * groups + 13]
+    s = lax.axis_index("section")
+    c = lax.axis_index("ctx")
+    t = lax.axis_index("tp")
+    chips = 16
+    rows = tokens.shape[1]
+    chip = c * 4 + t
+    cx = c + 1 - 2 * lax.rem(c, 2)
+    cy = lax.rem(c + 2, 4)
+    cd = 3 - c
+    sib = (1 - s, c, t)
+
+    def xor(k):
+        low = t + 1 - 2 * lax.rem(t, 2)
+        return {1: low, 2: lax.rem(t + 2, 4), 3: 3 - t}[k]
+
+    barrier = pltpu.get_barrier_semaphore()
+    for i in range(1, chips):
+        p = lax.rem(chip + i, chips)
+        pl.semaphore_signal(
+            barrier, 1, device_id=(s, p // 4, lax.rem(p, 4)), device_id_type=pl.DeviceIdType.MESH
+        )
+    for k in range(4):
+        where = (1 - s, c, t if k == 0 else xor(k))
+        pl.semaphore_signal(barrier, 1, device_id=where, device_id_type=pl.DeviceIdType.MESH)
+    pl.semaphore_wait(barrier, chips - 1 + 4)
+
+    def token_copy(i):
+        p = lax.rem(chip + i, chips)
+        return p, remote(
+            tokens.at[:, jnp.minimum(p, rows - 1)],
+            placed.at[:, chip],
+            t_send.at[i],
+            t_recv.at[i],
+            (s, p // 4, lax.rem(p, 4)),
+        )
+
+    for i in range(1, chips):
+        p, copy = token_copy(i)
+        pl.when(p < rows)(copy.start)
+    bring = pltpu.make_async_copy(
+        tokens.at[:, jnp.minimum(chip, rows - 1)], token_store, t_recv.at[0]
+    )
+    keep = pltpu.make_async_copy(token_store, placed.at[:, chip], t_send.at[0])
+    bring.start()
+
+    def block(g, who, h, q, u=None):
+        size = shards[g].shape[0]
+        start = h * (size // 2) + q * (size // 8)
+        length = size // 8
+        if u is not None:
+            length = size // 16
+            start = start + u * length
+        return outs[g].at[who, pl.ds(pl.multiple_of(start, 16), length)]
+
+    def z_copy(g, k, h):
+        size = shards[g].shape[0]
+        start = h * (size // 2) + c * (size // 8)
+        return remote(
+            shards[g].at[pl.ds(pl.multiple_of(start, 16), size // 8)],
+            block(g, t, h, c),
+            z_send.at[g, k - 1, h],
+            z_recv.at[g, k - 1],
+            (h, c, xor(k)),
+        )
+
+    def own_copies(g):
+        return (
+            pltpu.make_async_copy(shards[g], stores[g], own_sem.at[g, 3]),
+            pltpu.make_async_copy(stores[g], outs[g].at[t], own_sem.at[g, 0]),
+            remote(
+                shards[g], outs[g].at[t], own_sem.at[g, 1], own_sem.at[g, 2], sib
+            ),
+        )
+
+    items = [(g, k) for g in range(groups) for k in (1, 2, 3)]
+    mine = s == entry
+
+    def start_z(i):
+        g, k = items[i]
+
+        @pl.when(mine)
+        def _():
+            if k == 1:
+                fetch, _, far = own_copies(g)
+                fetch.start()
+                far.start()
+            for h in range(2):
+                z_copy(g, k, h).start()
+
+    def spread_copies(g, k):
+        who = xor(k)
+        src = block(g, who, s, c)
+        return (
+            remote(src, src, n_send.at[g, k - 1, 0], n_recv.at[g, k - 1, 0], (s, cx, t)),
+            remote(src, src, n_send.at[g, k - 1, 1], n_recv.at[g, k - 1, 1], (s, cy, t)),
+            sibling_copy(g, k, 0),
+        )
+
+    def sibling_copy(g, k, j):
+        q = (c, cx, cy, cd)[j]
+        src = block(g, xor(k), s, q)
+        return remote(src, src, s_send.at[g, k - 1, j], s_recv.at[g, k - 1, j], sib)
+
+    def forward_copies(g, k):
+        x_got = block(g, xor(k), s, cx, 0)
+        y_got = block(g, xor(k), s, cy, 1)
+        return (
+            remote(x_got, x_got, f_send.at[g, k - 1, 0], f_recv.at[g, k - 1, 0], (s, cy, t)),
+            remote(y_got, y_got, f_send.at[g, k - 1, 1], f_recv.at[g, k - 1, 1], (s, cx, t)),
+        )
+
+    def got(region, sem):
+        remote(region, region, own_sem.at[0, 1], sem, sib).wait_recv()
+
+    def stage2(i):
+        g, k = items[i]
+        got(block(g, xor(k), s, c), z_recv.at[g, k - 1])
+        for copy in spread_copies(g, k):
+            copy.start()
+
+    def stage3(i):
+        g, k = items[i]
+        ways = forward_copies(g, k)
+        for j, q in ((0, cx), (1, cy)):
+            got(block(g, xor(k), s, q), n_recv.at[g, k - 1, j])
+            ways[j].start()
+            sibling_copy(g, k, j + 1).start()
+
+    def stage4(i):
+        g, k = items[i]
+        for u in range(2):
+            got(block(g, xor(k), s, cd, u), f_recv.at[g, k - 1, u])
+        sibling_copy(g, k, 3).start()
+
+    count = len(items)
+    for i in range(min(window, count)):
+        start_z(i)
+    bring.wait()
+    keep.start()
+    lag = LAG
+    for step in range(count + 2 * lag):
+        if step < count:
+            stage2(step)
+            if step + window < count:
+                start_z(step + window)
+            if step % 3 == 2:
+
+                @pl.when(mine)
+                def _():
+                    fetch, local, _ = own_copies(step // 3)
+                    fetch.wait()
+                    local.start()
+
+        if 0 <= step - lag < count:
+            stage3(step - lag)
+        if 0 <= step - 2 * lag < count:
+            stage4(step - 2 * lag)
+
+    for g, k in items:
+        for j, q in enumerate((c, cx, cy, cd)):
+            got(block(g, xor(k), 1 - s, q), s_recv.at[g, k - 1, j])
+        for copy in spread_copies(g, k) + forward_copies(g, k):
+            copy.wait_send()
+        for j in (1, 2, 3):
+            sibling_copy(g, k, j).wait_send()
+
+    @pl.when(mine)
+    def _():
+        for g in range(groups):
+            _, local, far = own_copies(g)
+            local.wait()
+            far.wait_send()
+        for g, k in items:
+            for h in range(2):
+                z_copy(g, k, h).wait_send()
+
+    @pl.when(jnp.logical_not(mine))
+    def _():
+        for g in range(groups):
+            got(outs[g].at[t], own_sem.at[g, 2])
+
+    keep.wait()
+    for i in range(1, chips):
+        p, copy = token_copy(i)
+        pl.when(p < rows)(copy.wait_send)
+
+        @pl.when(chip < rows)
+        def _():
+            region = placed.at[:, lax.rem(chip + chips - i, chips)]
+            got(region, t_recv.at[i])
+
+
+LAG = 2
+
+
+def gather_call(entry, shards, tokens, window=4):
+    groups = len(shards)
+    kinds, _, part, width = tokens.shape
+    dma = pltpu.SemaphoreType.DMA
+    anywhere = pl.BlockSpec(memory_space=pl.ANY)
+    sizes = [
+        (groups, 3, 2),
+        (groups, 3),
+        (groups, 3, 2),
+        (groups, 3, 2),
+        (groups, 3, 2),
+        (groups, 3, 2),
+        (groups, 3, 4),
+        (groups, 3, 4),
+        (groups, 4),
+        (16,),
+        (16,),
+    ]
+    result = pl.pallas_call(
+        functools.partial(gather_kernel, entry, groups, window),
+        in_specs=[anywhere] * (groups + 1),
+        out_specs=[anywhere] * (groups + 1),
+        out_shape=[jax.ShapeDtypeStruct((4,) + v.shape, v.dtype) for v in shards]
+        + [jax.ShapeDtypeStruct((kinds, 16, part, width), tokens.dtype)],
+        scratch_shapes=[dma(size) for size in sizes]
+        + [pltpu.VMEM(v.shape, v.dtype) for v in shards]
+        + [pltpu.VMEM((kinds, part, width), tokens.dtype)],
+        compiler_params=pltpu.CompilerParams(
+            collective_id=entry, has_side_effects=True, vmem_limit_bytes=24 * 2**20
+        ),
+        name="gather_%d" % entry,
+    )(*shards, tokens)
+    return result[:groups], result[groups]
+
+
+def gather_plain(entry, shards):
+    full = [lax.all_gather(lax.all_gather(v, "tp"), "section") for v in shards]
+    return [v[entry] for v in full]
 
 
 def spread(blocks):
@@ -330,7 +589,45 @@
     stacked = jnp.stack(
         [pick(low, other), pick(other, high), pick(grads[:, :half], grads[:, half:])]
     )
-    source, target, cotangent = spread(stacked)
+    tail_rows = adapter_out[0].T
+    biases = jnp.concatenate([adapter_in_bias[0], adapter_out_bias[0]])
+    lanes = adapter_in_bias.shape[1]
+    biases = jnp.pad(biases.reshape(-1, lanes), ((0, 256 - biases.size // lanes), (0, 0)))
+    shards = [
+        jnp.concatenate([qkv_weights[0], out_weights], axis=0).reshape(-1, out_weights.shape[2]),
+        ffn_in[0],
+        jnp.concatenate([adapter_in[0], tail_rows], axis=1),
+        ffn_out[0],
+        cross_weights[0].reshape(-1, cross_weights.shape[3]),
+        biases,
+    ]
+    if lax.axis_size("ctx") == 4 and tp == 4:
+        enc_w, placed = gather_call(0, shards, stacked[:1])
+        source = placed.reshape(length, width)
+        dec_w, placed = gather_call(1, shards, stacked[1:])
+        target, cotangent = placed.reshape(2, length, width)
+    else:
+        source, target, cotangent = spread(stacked)
+        enc_w, dec_w = gather_plain(0, shards), gather_plain(1, shards)
+
+    def unpack(full):
+        attn, w_in, adapter, w_out, cross, bias = full
+        cols = lanes
+        attn = attn.reshape(tp, 4, -1, attn.shape[2])
+        cross = cross.reshape(tp, 2, -1, cross.shape[2])
+        b_out = bias[0, 1 : 1 + width // cols].reshape(width)
+        tail = (
+            w_in,
+            w_out,
+            adapter[:, :, :cols],
+            bias[:, 0],
+            adapter[:, :, cols:],
+            b_out,
+        )
+        return attn, cross, tail
+
+    enc_attn, enc_cross, enc_tail_w = unpack(enc_w)
+    dec_attn, dec_cross, dec_tail_w = unpack(dec_w)
 
     def ids_of(segments):
         flat = lax.all_gather(
@@ -359,53 +656,37 @@
     dec_ids = id_arrays(tgt_ids, tgt_ids)
     cross_ids = id_arrays(tgt_ids, src_ids)
 
-    w_attn, w_cross, w_in, w_out, a_in, b_in, a_out = gather_weights(
-        [
-            jnp.concatenate([qkv_weights[0], out_weights], axis=0),
-            cross_weights[0],
-            ffn_in[0],
-            ffn_out[0],
-            adapter_in[0],
-            adapter_in_bias[0],
-            adapter_out[0],
-        ]
-    )
-    b_out = lax.all_gather(adapter_out_bias[0], "section")
-    tails = [
-        (w_in[e], w_out[e], a_in[e], b_in[e], a_out[e], b_out[e]) for e in range(2)
-    ]
-
     enc_mid, enc_self = self_forward(
-        source, source.astype(F32), w_attn[0], enc_ids, False
-    )
-    encoded, enc_tail = tail_forward(enc_mid, tails[0])
+        source, source.astype(F32), enc_attn, enc_ids, False
+    )
+    encoded, enc_tail = tail_forward(enc_mid, enc_tail_w)
     encoded_bf = encoded.astype(BF16)
-    memory = [project(encoded_bf, w_cross[0, :, j]).astype(BF16) for j in range(2)]
+    memory = [project(encoded_bf, enc_cross[:, j]).astype(BF16) for j in range(2)]
     memory_other = swap(jnp.stack(memory))
     mem_keys = (memory[0], memory_other[0], memory[1], memory_other[1])
 
     dec_mid, dec_self = self_forward(
-        target, target.astype(F32), w_attn[1], dec_ids, True
-    )
-    queries = project(dec_mid.astype(BF16), w_cross[1, :, 0]).astype(BF16)
+        target, target.astype(F32), dec_attn, dec_ids, True
+    )
+    queries = project(dec_mid.astype(BF16), dec_cross[:, 0]).astype(BF16)
     cross_o, cross_lse = attention_forward(
         queries, *mem_keys, *cross_ids[0], False
     )
-    second, second_rstd = norm(dec_mid + unproject(cross_o, w_cross[1, :, 1]))
-    decoded, dec_tail = tail_forward(second, tails[1])
-
-    grad_second, dec_terms = tail_backward(cotangent.astype(F32), dec_tail, tails[1])
+    second, second_rstd = norm(dec_mid + unproject(cross_o, dec_cross[:, 1]))
+    decoded, dec_tail = tail_forward(second, dec_tail_w)
+
+    grad_second, dec_terms = tail_backward(cotangent.astype(F32), dec_tail, dec_tail_w)
     grad_cross = norm_back(second, second_rstd, grad_second)
-    do = project(grad_cross.astype(BF16), w_cross[1, :, 1]).astype(BF16)
+    do = project(grad_cross.astype(BF16), dec_cross[:, 1]).astype(BF16)
     dqc, dmk, dmv = attend_back(
         queries, mem_keys, cross_o, do, cross_lse, cross_ids, False
     )
-    grad_first = unproject(dqc, w_cross[1, :, 0]) + grad_cross
-    grad_target = self_backward(grad_first, dec_self, w_attn[1], dec_ids, True)
-
-    grad_encoded = unproject(dmk, w_cross[0, :, 0]) + unproject(dmv, w_cross[0, :, 1])
-    grad_mid, enc_terms = tail_backward(grad_encoded, enc_tail, tails[0])
-    grad_source = self_backward(grad_mid, enc_self, w_attn[0], enc_ids, False)
+    grad_first = unproject(dqc, dec_cross[:, 0]) + grad_cross
+    grad_target = self_backward(grad_first, dec_self, dec_attn, dec_ids, True)
+
+    grad_encoded = unproject(dmk, enc_cross[:, 0]) + unproject(dmv, enc_cross[:, 1])
+    grad_mid, enc_terms = tail_backward(grad_encoded, enc_tail, enc_tail_w)
+    grad_source = self_backward(grad_mid, enc_self, enc_attn, enc_ids, False)
 
     has_row = chip < row_count
 

time: 1310 us -> 941 us (0.72)
  waiting for transfers between devices: 759 us -> 123 us
  Pallas kernels: 153 us -> 458 us
  blocking collectives: 94.7 us -> 74 us
  matrix products: 174 us -> 157 us
    all_gather x12 -> x0, waiting for transfers between devices: 631 us -> none  [one(): return lax.all_gather(lax.all_gather(shard, 'tp'), 'section')]
    pallas_call x0 -> x2, Pallas kernels: none -> 305 us  [gather_call(): pl.pallas_call(functools.partial(gather_kernel, entry, groups, window), i...]
    dot_general x16, matrix products: 73.4 us -> 47.5 us  [project(): return jnp.einsum('pk,tkm->tpm', rows, weight, preferred_element_type=F32)]
    dot_general x16, matrix products: 68 us -> 93.2 us  [unproject(): return jnp.einsum('tpm,tkm->pk', blocks, weight, preferred_element_type=F32)]
    unnamed x190 -> x210, local copies, waits for them, and re-layouts: 15.6 us -> 36 us
    all_gather x3 -> x0, blocking collectives: 20.3 us -> none  [the longest x2 18 us: one(): return lax.all_gather(lax.all_gather(shard, 'tp'), 'section')]
  transfers between devices with their start and end apart: 30 -> 17, of which waited for: 14 -> 3; matrix products, arithmetic and copies ran while one was open for 13% -> 14% of each run, Pallas kernels for 8% -> 29%
where the time goes in v2:
time: 941 us; the launch traced here: 933 us
  Pallas kernels  458 us (49%)
  matrix products  157 us (17%)
  waiting for transfers between devices  123 us (13%)
  blocking collectives  74 us (8%)
  local copies, waits for them, and re-layouts  48.8 us (5%)
  other arithmetic  39 us (4%)
  starting transfers between devices  17.1 us (2%)
  between operations  15.7 us (2%)
    pallas_call x2, Pallas kernels, gather_call(): pl.pallas_call(functools.partial(gather_kernel, entry, groups, window), i...  305 us
    all_to_all x1, waiting for transfers between devices, collect(): moved = lax.all_to_all(blocks, ('ctx', 'tp'), 0, 0, tiled=True)  118 us
    dot_general x16, matrix products, unproject(): return jnp.einsum('tpm,tkm->pk', blocks, weight, preferred_element_type=F32)  93.2 us
    pallas_call x3, Pallas kernels, attention_backward(): pl.pallas_call(functools.partial(attn_bwd_kernel, causal), grid=(groups,)...  89.4 us
    pallas_call x3, Pallas kernels, attention_forward(): pl.pallas_call(functools.partial(attn_fwd_kernel, causal), grid=(groups,)...  63.3 us
    dot_general x16, matrix products, project(): return jnp.einsum('pk,tkm->tpm', rows, weight, preferred_element_type=F32)  47.5 us
    psum x1, blocking collectives, per_device(): bias_sum = lax.psum(sums[3], ('ctx', 'tp')).astype(F32)  40.6 us
    unnamed x210, local copies, waits for them, and re-layouts  36 us
  transfers between devices with their start and end apart: 17, of which 3 were waited for; matrix products, arithmetic and copies ran while one was open for 14% of the time, Pallas kernels for 29%

profile of v2, /device:TPU:0, one launch (start us, length us, event | category | flops | bytes accessed | tf_op | source)
XLA Modules:
  0.0 933.1 jit_solution(11623660568126701568)
XLA Ops:
  9.4 9.3 all_gather.6
  18.8 8.2 all_gather.7
  35.1 137.0 %gather_0.1 = (bf16[4,4096,256]{2,1,0:T(8,128)(2,1)S(1)}, bf16[4,1024,1024]{2,1,0:T(8,128)(2,1)}, bf16[4,1024,256]{2,1,0:T(8,128)(2,1)S(1)}, bf16[4,1024,1024]{2...) custom-call(bf16[4096,256]{1,0:T(8,128)(2,1)S(1)} %bitcast.578, ...), custom_call_target="tpu_custom_call" | custom-call | tf_op jit(solution)/shard_map/gather_0/pallas_call | solution.py:516
  180.1 168.4 %gather_1.1 = (bf16[4,4096,256]{2,1,0:T(8,128)(2,1)S(1)}, bf16[4,1024,1024]{2,1,0:T(8,128)(2,1)}, bf16[4,1024,256]{2,1,0:T(8,128)(2,1)S(1)}, bf16[4,1024,1024]{2...) custom-call(bf16[4096,256]{1,0:T(8,128)(2,1)S(1)} %bitcast.579, ...), custom_call_target="tpu_custom_call" | custom-call | tf_op jit(solution)/shard_map/gather_1/pallas_call | solution.py:516
  359.3 3.2 fusion.110.q_ref
  362.5 3.0 slice_bitcast_fusion.96
  365.5 21.0 %attn_fwd.3 = (bf16[4,512,256]{2,1,0:T(8,128)(2,1)S(1)}, f32[4,4,512]{2,1,0:T(4,128)S(1)}) custom-call(bf16[4,512,256]{2,1,0:T(8,128)(2,1)S(1)} %fusion.110.q_ref, bf16[4,512,256]{2,1,0:T(8,128)(2,1)S(1)} %bitcast.581, bf16[4,512,256]{2,1,0:T(8,128)(2,1)S(1)} %get-tuple-element.127.kx_ref, bf16[4,512,256]{2,1,0:T(8,128)(2,1)S(1)} %bitcast.584, ...), custom_call_target="tpu_custom_call" | custom-call | tf_op jit(solution)/shard_map/attn_fwd/pallas_call | solution.py:81
  386.6 3.3 fusion.194
  390.6 8.7 fusion.202
  402.9 5.0 fusion.195
  418.2 3.1 slice_bitcast_fusion.94
  421.3 21.4 %attn_fwd.4 = (bf16[4,512,256]{2,1,0:T(8,128)(2,1)S(1)}, f32[4,4,512]{2,1,0:T(4,128)S(1)}) custom-call(bf16[4,512,256]{2,1,0:T(8,128)(2,1)S(1)} %fusion.112.q_ref, bf16[4,512,256]{2,1,0:T(8,128)(2,1)S(1)} %bitcast.591, bf16[4,512,256]{2,1,0:T(8,128)(2,1)S(1)} %get-tuple-element.129.kx_ref, bf16[4,512,256]{2,1,0:T(8,128)(2,1)S(1)} %bitcast.588, ...), custom_call_target="tpu_custom_call" | custom-call | tf_op jit(solution)/shard_map/attn_fwd/pallas_call | solution.py:81
  442.7 3.4 fusion.193
  449.1 21.0 %attn_fwd.5 = (bf16[4,512,256]{2,1,0:T(8,128)(2,1)S(1)}, f32[4,4,512]{2,1,0:T(4,128)S(1)}) custom-call(bf16[4,512,256]{2,1,0:T(8,128)(2,1)S(1)} %fusion.114.q_ref, bf16[4,512,256]{2,1,0:T(8,128)(2,1)S(1)} %bitcast.596, bf16[4,512,256]{2,1,0:T(8,128)(2,1)S(1)} %get-tuple-element.125.kx_ref, bf16[4,512,256]{2,1,0:T(8,128)(2,1)S(1)} %bitcast.593, ...), custom_call_target="tpu_custom_call" | custom-call | tf_op jit(solution)/shard_map/attn_fwd/pallas_call | solution.py:81
  472.2 8.3 fusion.203
  483.8 5.0 fusion.197
  496.9 28.7 %fusion.191 = (f32[512]{0:T(512)S(1)}, f32[512]{0:T(512)S(1)}, f32[512,1024]{1,0:T(8,128)}) fusion(f32[512]{0:T(512)S(1)} %add_rsqrt_fusion.1, f32[512,1024]{1,0:T(8,128)S(1)} %get-tuple-element.141, f32[512]{0:T(512)S(1)} %broadcast_multiply_fusion.11, f32[512,1024]{1,0:T(8,128)} %copy-done.65, f32[512,1024,1]{1,0,2:T(8,128)} %fusion.158, ...), kind=kOutput, calls=%fused_computation.330 | convolution fusion | flops 8619294720 | bytes 33562624 | tf_op jit(solution)/shard_map/tpm,tkm->pk/dot_general | solution.py:200
  525.6 4.7 fusion.115.do_ref
  530.4 31.1 %attn_bwd.3 = (bf16[4,512,256]{2,1,0:T(8,128)(2,1)S(1)}, bf16[4,512,256]{2,1,0:T(8,128)(2,1)S(1)}, bf16[4,512,256]{2,1,0:T(8,128)(2,1)S(1)}, bf16[4,512,256]{2,1,0:T(8,128)(2,1)S(1)}, bf16[4,512,256]{2,1,0:T(8,128)(2,1)S(1)}) custom-call(bf16[4,512,256]{2,1,0:T(8,128)(2,1)} %copy-done.18, bf16[4,512,256]{2,1,0:T(8,128)(2,1)} %bitcast.597, ...), custom_call_target="tpu_custom_call" | custom-call | tf_op jit(solution)/shard_map/attn_bwd/pallas_call | solution.py:164
  563.7 5.6 fusion.190
  569.4 4.8 fusion.113.do_ref
  574.1 27.1 %attn_bwd.5 = (bf16[4,512,256]{2,1,0:T(8,128)(2,1)S(1)}, bf16[4,512,256]{2,1,0:T(8,128)(2,1)S(1)}, bf16[4,512,256]{2,1,0:T(8,128)(2,1)S(1)}, bf16[4,512,256]{2,1,0:T(8,128)(2,1)S(1)}, bf16[4,512,256]{2,1,0:T(8,128)(2,1)S(1)}) custom-call(bf16[4,512,256]{2,1,0:T(8,128)(2,1)} %copy-done.17, bf16[4,512,256]{2,1,0:T(8,128)(2,1)} %bitcast.590, ...), custom_call_target="tpu_custom_call" | custom-call | tf_op jit(solution)/shard_map/attn_bwd/pallas_call | solution.py:164
  616.0 28.5 %fusion.188 = (f32[512]{0:T(512)S(1)}, f32[512]{0:T(512)S(1)}, f32[512,1024]{1,0:T(8,128)}) fusion(f32[512]{0:T(512)S(1)} %add_rsqrt_fusion.4, f32[512,1024]{1,0:T(8,128)S(1)} %copy-done.51, f32[512]{0:T(512)S(1)} %broadcast_multiply_fusion.14, f32[512,1024]{1,0:T(8,128)} %copy-done.67, f32[512,1024,1]{1,0,2:T(8,128)} %fusion.164, ...), kind=kOutput, calls=%fused_computation.327 | convolution fusion | flops 8619294720 | bytes 33562624 | tf_op jit(solution)/shard_map/tpm,tkm->pk/dot_general | solution.py:200
  644.6 4.7 fusion.111.do_ref
  649.3 31.3 %attn_bwd.4 = (bf16[4,512,256]{2,1,0:T(8,128)(2,1)S(1)}, bf16[4,512,256]{2,1,0:T(8,128)(2,1)S(1)}, bf16[4,512,256]{2,1,0:T(8,128)(2,1)S(1)}, bf16[4,512,256]{2,1,0:T(8,128)(2,1)S(1)}, bf16[4,512,256]{2,1,0:T(8,128)(2,1)S(1)}) custom-call(bf16[4,512,256]{2,1,0:T(8,128)(2,1)} %copy-done.16, bf16[4,512,256]{2,1,0:T(8,128)(2,1)} %bitcast.582, ...), custom_call_target="tpu_custom_call" | custom-call | tf_op jit(solution)/shard_map/attn_bwd/pallas_call | solution.py:164
  682.5 3.0 fusion.72
  695.1 3.9 fusion.50
  707.3 13.9 %all-to-all-start = ((bf16[16,4,32,1024]{3,2,1,0:T(8,128)(2,1)}), bf16[16,4,32,1024]{3,2,1,0:T(8,128)(2,1)}, u32[]{:S(2)}, u32[]{:S(2)}) async-start(bf16[16,4,32,1024]{3,2,1,0:T(8,128)(2,1)} %maximum_bitcast_fusion), calls=%async_computation | async-start | bytes 8388608 | tf_op jit(solution)/shard_map/all_to_all | solution.py:553
  735.7 117.6 %all-to-all-done = bf16[16,4,32,1024]{3,2,1,0:T(8,128)(2,1)} async-done(((bf16[16,4,32,1024]{3,2,1,0:T(8,128)(2,1)}), bf16[16,4,32,1024]{3,2,1,0:T(8,128)(2,1)}, u32[]{:S(2)}, u32[]{:S(2)}) %all-to-all-start) | async-done | bytes 4194336 | tf_op jit(solution)/shard_map/all_to_all | solution.py:553
  858.6 8.4 all-reduce.1
  867.7 7.6 psum.29
  875.8 40.6 %psum.31 = bf16[1,1024]{1,0:T(2,128)(2,1)S(1)} all-reduce(bf16[1,1024]{1,0:T(2,128)(2,1)S(1)} %broadcast_in_dim.75), channel_id=1, replica_groups=mesh['section'=2,'ctx'=4,'tp'=4] {'ctx','tp'}, use_global_device_ids=true, to_apply=%region_30.31 | all-reduce | flops 1024 | bytes 4096 | tf_op jit(solution)/shard_map/psum | solution.py:704
  (369 shorter events, 126.8 us)
Async XLA Ops:
  7.2 22.5 %copy-start.85 = (bf16[1,1024]{1,0:T(2,128)(2,1)S(1)}, bf16[1,1024]{1,0:T(2,128)(2,1)}, u32[]{:S(2)}) copy-start(bf16[1,1024]{1,0:T(2,128)(2,1)} %param.25) | copy-start | bytes 6148
  7.2 22.6 %copy-start.86 = (bf16[1,128]{1,0:T(2,128)(2,1)S(1)}, bf16[1,128]{1,0:T(2,128)(2,1)}, u32[]{:S(2)}) copy-start(bf16[1,128]{1,0:T(2,128)(2,1)} %param.23) | copy-start | bytes 772
  7.2 23.6 %copy-start.70 = (bf16[1,3,1024,256]{3,2,1,0:T(8,128)(2,1)S(1)}, bf16[1,3,1024,256]{3,2,1,0:T(8,128)(2,1)}, u32[]{:S(2)}) copy-start(bf16[1,3,1024,256]{3,2,1,0:T(8,128)(2,1)} %param.17) | copy-start | bytes 4718596
  7.2 23.6 %copy-start.81 = (bf16[1,1024,256]{2,1,0:T(8,128)(2,1)S(1)}, bf16[1,1024,256]{2,1,0:T(8,128)(2,1)}, u32[]{:S(2)}) copy-start(bf16[1,1024,256]{2,1,0:T(8,128)(2,1)} %param.18) | copy-start | bytes 1572868
  8.9 23.5 %collective-permute-start = (bf16[12,32,1024]{2,1,0:T(8,128)(2,1)S(1)}, bf16[12,32,1024]{2,1,0:T(8,128)(2,1)}, u32[]{:S(2)}, u32[]{:S(2)}) collective-permute-start(bf16[12,32,1024]{2,1,0:T(8,128)(2,1)S(1)} %broadcast_select_fusion.3), channel_id=1, source_target_pairs={{0,16},{16,0},{1,17},{17,1},{2,18},{18,2},{3,19},{19,3},{4,20},{20... | collective-permute-start | bytes 2359304 | tf_op jit(solution)/shard_map/ppermute | solution.py:19
  175.4 190.1 %copy-start = (bf16[4,256,512]{1,2,0:T(8,128)(2,1)}, bf16[4,256,512]{1,2,0:T(8,128)(2,1)S(1)}, u32[]{:S(2)}) copy-start(bf16[4,256,512]{1,2,0:T(8,128)(2,1)S(1)} %fusion.108) | copy-start | bytes 3145732
  178.3 187.3 %copy-start.1 = (bf16[4,256,512]{1,2,0:T(8,128)(2,1)}, bf16[4,256,512]{1,2,0:T(8,128)(2,1)S(1)}, u32[]{:S(2)}) copy-start(bf16[4,256,512]{1,2,0:T(8,128)(2,1)S(1)} %fusion.107) | copy-start | bytes 3145732
  179.9 182.6 %collective-permute-start.1 = (bf16[2,4,512,256]{3,2,1,0:T(8,128)(2,1)}, bf16[2,4,512,256]{3,2,1,0:T(8,128)(2,1)}, u32[]{:S(2)}, u32[]{:S(2)}) collective-permute-start(bf16[2,4,512,256]{3,2,1,0:T(8,128)(2,1)} %pad_maximum_fusion.1), channel_id=1, source_target_pairs={{0,16},{16,0},{1,17},{17,1},{2,18},{18,2},{3,19},{19,3},{4,20},{20... | collective-permute-start | bytes 6291464 | tf_op jit(solution)/shard_map/ppermute | solution.py:19
  358.5 59.7 %collective-permute-start.2 = (bf16[2,4,512,256]{3,2,1,0:T(8,128)(2,1)}, bf16[2,4,512,256]{3,2,1,0:T(8,128)(2,1)}, u32[]{:S(2)}, u32[]{:S(2)}) collective-permute-start(bf16[2,4,512,256]{3,2,1,0:T(8,128)(2,1)} %pad_maximum_fusion.2), channel_id=1, source_target_pairs={{0,16},{16,0},{1,17},{17,1},{2,18},{18,2},{3,19},{19,3},{4,20},{20... | collective-permute-start | bytes 6291464 | tf_op jit(solution)/shard_map/ppermute | solution.py:19
  365.5 21.1 %copy-start.2 = (bf16[4,512,256]{2,1,0:T(8,128)(2,1)}, bf16[4,512,256]{2,1,0:T(8,128)(2,1)S(1)}, u32[]{:S(2)}) copy-start(bf16[4,512,256]{2,1,0:T(8,128)(2,1)S(1)} %get-tuple-element.127.kx_ref) | copy-start | bytes 3145732
  365.5 21.0 %copy-start.45 = (bf16[1,16,32,1024]{3,2,1,0:T(8,128)(2,1)S(1)}, bf16[1,16,32,1024]{3,2,1,0:T(8,128)(2,1)}, u32[]{:S(2)}) copy-start(bf16[1,16,32,1024]{3,2,1,0:T(8,128)(2,1)} %copy-done.44) | copy-start | bytes 3145732
  412.4 36.6 %copy-start.8 = (bf16[4,256,512]{1,2,0:T(8,128)(2,1)}, bf16[4,256,512]{1,2,0:T(8,128)(2,1)S(1)}, u32[]{:S(2)}) copy-start(bf16[4,256,512]{1,2,0:T(8,128)(2,1)S(1)} %fusion.99) | copy-start | bytes 3145732
  413.7 35.4 %copy-start.9 = (bf16[4,256,512]{1,2,0:T(8,128)(2,1)}, bf16[4,256,512]{1,2,0:T(8,128)(2,1)S(1)}, u32[]{:S(2)}) copy-start(bf16[4,256,512]{1,2,0:T(8,128)(2,1)S(1)} %fusion.100) | copy-start | bytes 3145732
  413.9 33.9 %collective-permute-start.3 = (bf16[2,4,512,256]{3,2,1,0:T(8,128)(2,1)S(1)}, bf16[2,4,512,256]{3,2,1,0:T(8,128)(2,1)S(1)}, u32[]{:S(2)}, u32[]{:S(2)}) collective-permute-start(bf16[2,4,512,256]{3,2,1,0:T(8,128)(2,1)S(1)} %pad_maximum_fusion.3), channel_id=1, source_target_pairs={{0,16},{16,0},{1,17},{17,1},{2,18},{18,2},{3,19},{19,3},{4,20},{20... | collective-permute-start | bytes 6291464 | tf_op jit(solution)/shard_map/ppermute | solution.py:19
  421.3 21.4 %copy-start.7 = (bf16[4,512,256]{2,1,0:T(8,128)(2,1)}, bf16[4,512,256]{2,1,0:T(8,128)(2,1)S(1)}, u32[]{:S(2)}) copy-start(bf16[4,512,256]{2,1,0:T(8,128)(2,1)S(1)} %get-tuple-element.129.kx_ref) | copy-start | bytes 3145732
  446.1 24.0 %copy-start.53 = (f32[512,1024]{1,0:T(8,128)}, f32[512,1024]{1,0:T(8,128)S(1)}, u32[]{:S(2)}) copy-start(f32[512,1024]{1,0:T(8,128)S(1)} %get-tuple-element.135) | copy-start | bytes 6291460
  449.1 21.0 %copy-start.10 = (bf16[4,512,256]{2,1,0:T(8,128)(2,1)}, bf16[4,512,256]{2,1,0:T(8,128)(2,1)S(1)}, u32[]{:S(2)}) copy-start(bf16[4,512,256]{2,1,0:T(8,128)(2,1)S(1)} %get-tuple-element.125.kx_ref) | copy-start | bytes 3145732
  471.5 54.1 %copy-start.56 = (f32[512,1024]{1,0:T(8,128)}, f32[512,1024]{1,0:T(8,128)S(1)}, u32[]{:S(2)}) copy-start(f32[512,1024]{1,0:T(8,128)S(1)} %get-tuple-element.141) | copy-start | bytes 6291460
  563.4 40.2 %collective-permute-start.4 = (bf16[2,4,512,256]{3,2,1,0:T(8,128)(2,1)}, bf16[2,4,512,256]{3,2,1,0:T(8,128)(2,1)}, u32[]{:S(2)}, u32[]{:S(2)}) collective-permute-start(bf16[2,4,512,256]{3,2,1,0:T(8,128)(2,1)} %pad_maximum_fusion.4), channel_id=1, source_target_pairs={{0,16},{16,0},{1,17},{17,1},{2,18},{18,2},{3,19},{19,3},{4,20},{20... | collective-permute-start | bytes 6291464 | tf_op jit(solution)/shard_map/ppermute | solution.py:19
  603.2 82.3 %collective-permute-start.6 = (bf16[2,4,512,256]{3,2,1,0:T(8,128)(2,1)}, bf16[2,4,512,256]{3,2,1,0:T(8,128)(2,1)}, u32[]{:S(2)}, u32[]{:S(2)}) collective-permute-start(bf16[2,4,512,256]{3,2,1,0:T(8,128)(2,1)} %pad_maximum_fusion.6), channel_id=1, source_target_pairs={{0,16},{16,0},{1,17},{17,1},{2,18},{18,2},{3,19},{19,3},{4,20},{20... | collective-permute-start | bytes 6291464 | tf_op jit(solution)/shard_map/ppermute | solution.py:19
  649.3 38.4 %slice-start = ((s8[8388608]{0:T(1024)(128)(4,1)}), s8[4194304]{0:T(1024)(128)(4,1)S(1)}, s32[]{:S(2)}) async-start(s8[8388608]{0:T(1024)(128)(4,1)} %bitcast.625), calls=%async_computation.6 | async-start | bytes 8388608
  682.1 17.0 %collective-permute-start.5 = (bf16[2,4,512,256]{3,2,1,0:T(8,128)(2,1)}, bf16[2,4,512,256]{3,2,1,0:T(8,128)(2,1)}, u32[]{:S(2)}, u32[]{:S(2)}) collective-permute-start(bf16[2,4,512,256]{3,2,1,0:T(8,128)(2,1)} %pad_maximum_fusion.5), channel_id=1, source_target_pairs={{0,16},{16,0},{1,17},{17,1},{2,18},{18,2},{3,19},{19,3},{4,20},{20... | collective-permute-start | bytes 6291464 | tf_op jit(solution)/shard_map/ppermute | solution.py:19
  707.3 146.1 %all-to-all-start = ((bf16[16,4,32,1024]{3,2,1,0:T(8,128)(2,1)}), bf16[16,4,32,1024]{3,2,1,0:T(8,128)(2,1)}, u32[]{:S(2)}, u32[]{:S(2)}) async-start(bf16[16,4,32,1024]{3,2,1,0:T(8,128)(2,1)} %maximum_bitcast_fusion), calls=%async_computation | async-start | bytes 8388608 | tf_op jit(solution)/shard_map/all_to_all | solution.py:553
  721.2 137.4 %reduce-scatter.5.cloned.1.call-start = ((), (), s32[]{:S(2)}) async-start(), calls=%async_computation.4 | async-start | bytes 1310720 | tf_op jit(solution)/shard_map/reduce_scatter | solution.py:701
  724.0 2.7 collective-permute-start.11
  728.4 130.2 %reduce-scatter.3.cloned.1.call-start = ((), (), s32[]{:S(2)}) async-start(), calls=%async_computation.3 | async-start | bytes 1310720 | tf_op jit(solution)/shard_map/reduce_scatter | solution.py:701
  730.6 2.7 collective-permute-start.9
  735.0 182.0 %all-reduce.5.cloned.1.call-start = ((), (), s32[]{:S(2)}) async-start(), calls=%async_computation.5 | async-start | bytes 1048576 | tf_op jit(solution)/shard_map/psum | solution.py:703
  735.6 123.0 %collective-permute-start.10 = (bf16[4,128]{1,0:T(4,128)(2,1)S(1)}, bf16[4,128]{1,0:T(4,128)(2,1)S(1)}, u32[]{:S(2)}, u32[]{:S(2)}) collective-permute-start(bf16[4,128]{1,0:T(4,128)(2,1)S(1)} %broadcast_select_fusion.5), channel_id=1, source_target_pairs={{0,16},{16,0},{1,17},{17,1},{2,18},{18,2},{3,19},{19,3},{4,20},{20... | collective-permute-start | bytes 3080 | tf_op jit(solution)/shard_map/ppermute | solution.py:19
  858.0 62.7 %collective-permute-start.7 = (bf16[12,32,1024]{2,1,0:T(8,128)(2,1)S(1)}, bf16[12,32,1024]{2,1,0:T(8,128)(2,1)S(1)}, u32[]{:S(2)}, u32[]{:S(2)}) collective-permute-start(bf16[12,32,1024]{2,1,0:T(8,128)(2,1)S(1)} %get-tuple-element.119), channel_id=1, source_target_pairs={{0,16},{16,0},{1,17},{17,1},{2,18},{18,2},{3,19},{19,3},{4,20},{20... | collective-permute-start | bytes 2359304 | tf_op jit(solution)/shard_map/ppermute | solution.py:19
  858.0 62.7 %collective-permute-start.8 = (bf16[12,32,1024]{2,1,0:T(8,128)(2,1)S(1)}, bf16[12,32,1024]{2,1,0:T(8,128)(2,1)S(1)}, u32[]{:S(2)}, u32[]{:S(2)}) collective-permute-start(bf16[12,32,1024]{2,1,0:T(8,128)(2,1)S(1)} %get-tuple-element.118), channel_id=1, source_target_pairs={{0,16},{16,0},{1,17},{17,1},{2,18},{18,2},{3,19},{19,3},{4,20},{20... | collective-permute-start | bytes 2359304 | tf_op jit(solution)/shard_map/ppermute | solution.py:19
  858.5 17.3 %collective-permute-start.12 = (bf16[1024]{0:T(1024)(128)(2,1)S(1)}, bf16[1024]{0:T(1024)(128)(2,1)S(1)}, u32[]{:S(2)}, u32[]{:S(2)}) collective-permute-start(bf16[1024]{0:T(1024)(128)(2,1)S(1)} %broadcast_select_fusion.4), channel_id=1, source_target_pairs={{0,16},{16,0},{1,17},{17,1},{2,18},{18,2},{3,19},{19,3},{4,20},{20... | collective-permute-start | bytes 6152 | tf_op jit(solution)/shard_map/ppermute | solution.py:19
  (88 other events, 361.0 us)
Sparse Core Ops, SparseCore 0:
  728.5 67.7 reduce-scatter.4
  799.3 37.1 reduce-scatter.2
  858.7 42.3 all-reduce.4

commit v3 on v2

--- a/solution.py
+++ b/solution.py
@@ -19,6 +19,197 @@
     return lax.ppermute(value, "section", [(0, 1), (1, 0)])
 
 
+def remote(src, dst, send, recv, where):
+    return pltpu.make_async_remote_copy(
+        src_ref=src,
+        dst_ref=dst,
+        send_sem=send,
+        recv_sem=recv,
+        device_id=where,
+        device_id_type=pl.DeviceIdType.MESH,
+    )
+
+
+def device_of(section, chip):
+    return (section, chip // 4, lax.rem(chip, 4))
+
+
+def greet_all():
+    s = lax.axis_index("section")
+    chip = lax.axis_index("ctx") * 4 + lax.axis_index("tp")
+    barrier = pltpu.get_barrier_semaphore()
+    for core in (0, 1):
+        for i in range(core, 16):
+            pl.semaphore_signal(
+                barrier,
+                1,
+                device_id=device_of(lax.rem(s + 1 - core, 2), lax.rem(chip + i, 16)),
+                device_id_type=pl.DeviceIdType.MESH,
+            )
+    pl.semaphore_wait(barrier, 31)
+
+
+class Scatter:
+    BRING = 2
+
+    def __init__(self, arrays, rows, call_id):
+        self.inputs = [a for a, _ in arrays]
+        self.kinds = [k for _, k in arrays]
+        self.rows = rows
+        self.call_id = call_id
+        self.shapes = [
+            jax.ShapeDtypeStruct(
+                ((16,) if k == self.BRING else (rows, 2)) + a.shape[1:], a.dtype
+            )
+            for a, k in arrays
+        ]
+        count = len(arrays)
+        self.scratch = [
+            pltpu.SemaphoreType.DMA((count, 16)),
+            pltpu.SemaphoreType.DMA((count, 16, 2)),
+        ]
+
+    def sends(self, ins, outs, sems):
+        send, recv = sems
+        s = lax.axis_index("section")
+        chip = lax.axis_index("ctx") * 4 + lax.axis_index("tp")
+        for a, kind in enumerate(self.kinds):
+            for i in range(16):
+                p = lax.rem(chip + i, 16)
+                if kind == self.BRING:
+                    ready = p < self.rows
+                    src = ins[a].at[jnp.minimum(p, self.rows - 1)]
+                    dst = outs[a].at[chip]
+                    core, mark = s, 0
+                    stays = True
+                else:
+                    ready = chip < self.rows
+                    src = ins[a].at[p]
+                    dst = outs[a].at[jnp.minimum(chip, self.rows - 1), s]
+                    core, mark = kind, s
+                    stays = s == kind
+                near = pltpu.make_async_copy(src, dst, send.at[a, i])
+                far = remote(
+                    src, dst, send.at[a, i], recv.at[a, i, mark], device_of(core, p)
+                )
+                yield i, ready, stays, near, far
+
+    def start(self, ins, outs, sems):
+        greet_all()
+        for i, ready, stays, near, far in self.sends(ins, outs, sems):
+
+            @pl.when(ready)
+            def _():
+                if i:
+                    far.start()
+                elif stays is True:
+                    near.start()
+                else:
+                    pl.when(stays)(near.start)
+                    pl.when(jnp.logical_not(stays))(far.start)
+
+    def finish(self, ins, outs, sems):
+        send, recv = sems
+        s = lax.axis_index("section")
+        chip = lax.axis_index("ctx") * 4 + lax.axis_index("tp")
+        for i, ready, stays, near, far in self.sends(ins, outs, sems):
+
+            @pl.when(ready)
+            def _():
+                if i:
+                    far.wait_send()
+                elif stays is True:
+                    near.wait()
+                else:
+                    pl.when(stays)(near.wait)
+                    pl.when(jnp.logical_not(stays))(far.wait_send)
+
+        def got(region, sem):
+            remote(region, region, send.at[0, 0], sem, (1 - s, 0, 0)).wait_recv()
+
+        for a, kind in enumerate(self.kinds):
+            for i in range(16):
+                sender = lax.rem(chip + 16 - i, 16)
+                if kind == self.BRING:
+                    if i:
+
+                        @pl.when(chip < self.rows)
+                        def _():
+                            got(outs[a].at[sender], recv.at[a, i, 0])
+
+                    continue
+
+                @pl.when((s == kind) & (sender < self.rows))
+                def _():
+                    for core in (0, 1) if i else (1 - kind,):
+                        region = outs[a].at[jnp.minimum(sender, self.rows - 1), core]
+                        got(region, recv.at[a, i, core])
+
+
+def split_refs(rider, refs, own_outs):
+    count = len(rider.inputs) if rider else 0
+    mine = refs[count : count + own_outs]
+    outs = refs[count + own_outs : 2 * count + own_outs]
+    sems = refs[2 * count + own_outs :]
+    return mine, (refs[:count], outs, sems)
+
+
+def ride_start(rider, parts):
+    if rider:
+        pl.when(pl.program_id(0) == 0)(lambda: rider.start(*parts))
+
+
+def ride_finish(rider, parts):
+    if rider:
+        last = pl.num_programs(0) - 1
+        pl.when(pl.program_id(0) == last)(lambda: rider.finish(*parts))
+
+
+def send_kernel(rider, *refs):
+    n = len(rider.inputs)
+    block_in, (own, spread_out) = refs[n], (refs[n], refs[2 * n + 1])
+    ins, outs = refs[:n], refs[n + 1 : 2 * n + 1]
+    sems = refs[2 * n + 2 : 2 * n + 4]
+    b_send, b_recv = refs[2 * n + 4 :]
+    rider.start(ins, outs, sems)
+    s = lax.axis_index("section")
+    c = lax.axis_index("ctx")
+    t = lax.axis_index("tp")
+    dst = spread_out.at[c]
+    keep = pltpu.make_async_copy(own, dst, b_send.at[0])
+    keep.start()
+    ways = [
+        remote(own, dst, b_send.at[j], b_recv.at[j], (s, lax.rem(c + j, 4), t))
+        for j in (1, 2, 3)
+    ]
+    for way in ways:
+        way.start()
+    keep.wait()
+    for j, way in enumerate(ways):
+        way.wait_send()
+        region = spread_out.at[lax.rem(c + 3 - j, 4)]
+        remote(region, region, b_send.at[0], b_recv.at[j + 1], (s, c, t)).wait_recv()
+    rider.finish(ins, outs, sems)
+
+
+def send_call(rider, block):
+    anywhere = pl.BlockSpec(memory_space=pl.ANY)
+    count = len(rider.inputs)
+    result = pl.pallas_call(
+        functools.partial(send_kernel, rider),
+        in_specs=[anywhere] * (count + 1),
+        out_specs=[anywhere] * (count + 1),
+        out_shape=rider.shapes + [jax.ShapeDtypeStruct((4,) + block.shape, block.dtype)],
+        scratch_shapes=rider.scratch
+        + [pltpu.SemaphoreType.DMA((4,)), pltpu.SemaphoreType.DMA((4,))],
+        compiler_params=pltpu.CompilerParams(
+            collective_id=rider.call_id, has_side_effects=True
+        ),
+        name="send_last",
+    )(*rider.inputs, block)
+    return result[:count], result[count]
+
+
 def dot_nt(left, right, **kw):
     return lax.dot_general(
         left, right, (((1,), (1,)), ((), ())), preferred_element_type=F32, **kw
@@ -38,8 +229,10 @@
 
 
 def attn_fwd_kernel(
-    causal, q_ref, ko_ref, kx_ref, vo_ref, vx_ref, qi_ref, ki_ref, o_ref, lse_ref
+    causal, rider, q_ref, ko_ref, kx_ref, vo_ref, vx_ref, qi_ref, ki_ref, *rest
 ):
+    (o_ref, lse_ref), parts_ride = split_refs(rider, rest, 2)
+    ride_start(rider, parts_ride)
     length = q_ref.shape[1]
     heads = q_ref.shape[2] // HEAD
     block = length // 2
@@ -72,32 +265,49 @@
             o_ref[0, rows, cols] = (out / total).astype(BF16)
             lse = top + jnp.log(total)
             lse_ref[0, h : h + 1, rows] = jnp.broadcast_to(lse, (block, 128)).T[0:1]
-
-
-def attention_forward(q, k_own, k_oth, v_own, v_oth, qi, ki, causal):
+    ride_finish(rider, parts_ride)
+
+
+def attention_call(kernel, name, causal, rider, blocks, small, outs):
+    groups = blocks[0].shape[0]
+    anywhere = pl.BlockSpec(memory_space=pl.ANY)
+    extra = rider.inputs if rider else []
+    params = {"vmem_limit_bytes": 48 * 2**20}
+    if rider:
+        params.update(collective_id=rider.call_id, has_side_effects=True)
+
+    def group_spec(shape):
+        return pl.BlockSpec((1,) + shape[1:], lambda t: (t, 0, 0))
+
+    result = pl.pallas_call(
+        functools.partial(kernel, causal, rider),
+        grid=(groups,),
+        in_specs=[group_spec(v.shape) for v in blocks]
+        + [pl.BlockSpec(v.shape, lambda t: (0, 0)) for v in small]
+        + [anywhere] * len(extra),
+        out_specs=[group_spec(v.shape) for v in outs] + [anywhere] * len(extra),
+        out_shape=outs + (rider.shapes if rider else []),
+        scratch_shapes=rider.scratch if rider else [],
+        compiler_params=pltpu.CompilerParams(**params),
+        name=name,
+    )(*blocks, *small, *extra)
+    return result[: len(outs)], result[len(outs) :]
+
+
+def attention_forward(q, keys, ids, causal, rider=None):
     groups, length, width = q.shape
-    heads = width // HEAD
-    spec = pl.BlockSpec((1, length, width), lambda t: (t, 0, 0))
-    return pl.pallas_call(
-        functools.partial(attn_fwd_kernel, causal),
-        grid=(groups,),
-        in_specs=[spec] * 5
-        + [
-            pl.BlockSpec(qi.shape, lambda t: (0, 0)),
-            pl.BlockSpec(ki.shape, lambda t: (0, 0)),
-        ],
-        out_specs=[spec, pl.BlockSpec((1, heads, length), lambda t: (t, 0, 0))],
-        out_shape=[
-            jax.ShapeDtypeStruct(q.shape, BF16),
-            jax.ShapeDtypeStruct((groups, heads, length), F32),
-        ],
-        compiler_params=pltpu.CompilerParams(vmem_limit_bytes=48 * 2**20),
-        name="attn_fwd",
-    )(q, k_own, k_oth, v_own, v_oth, qi, ki)
+    outs = [
+        jax.ShapeDtypeStruct(q.shape, BF16),
+        jax.ShapeDtypeStruct((groups, width // HEAD, length), F32),
+    ]
+    return attention_call(
+        attn_fwd_kernel, "attn_fwd", causal, rider, [q, *keys], ids, outs
+    )
 
 
 def attn_bwd_kernel(
     causal,
+    rider,
     q_ref,
     ko_ref,
     kx_ref,
@@ -108,12 +318,10 @@
     lse_ref,
     qi_ref,
     ki_ref,
-    dq_ref,
-    dko_ref,
-    dkx_ref,
-    dvo_ref,
-    dvx_ref,
+    *rest,
 ):
+    (dq_ref, dko_ref, dkx_ref, dvo_ref, dvx_ref), parts_ride = split_refs(rider, rest, 5)
+    ride_start(rider, parts_ride)
     length = q_ref.shape[1]
     heads = q_ref.shape[2] // HEAD
     block = length // 2
@@ -155,26 +363,14 @@
                     dq[1] = dq[1] + part[block:]
         dq_ref[0, :block, cols] = (dq[0] * SCALE).astype(BF16)
         dq_ref[0, block:, cols] = (dq[1] * SCALE).astype(BF16)
-
-
-def attention_backward(q, k_own, k_oth, v_own, v_oth, o, do, lse, qi, ki, causal):
-    groups, length, width = q.shape
-    heads = width // HEAD
-    spec = pl.BlockSpec((1, length, width), lambda t: (t, 0, 0))
-    return pl.pallas_call(
-        functools.partial(attn_bwd_kernel, causal),
-        grid=(groups,),
-        in_specs=[spec] * 7
-        + [
-            pl.BlockSpec((1, heads, length), lambda t: (t, 0, 0)),
-            pl.BlockSpec(qi.shape, lambda t: (0, 0)),
-            pl.BlockSpec(ki.shape, lambda t: (0, 0)),
-        ],
-        out_specs=[spec] * 5,
-        out_shape=[jax.ShapeDtypeStruct(q.shape, BF16)] * 5,
-        compiler_params=pltpu.CompilerParams(vmem_limit_bytes=48 * 2**20),
-        name="attn_bwd",
-    )(q, k_own, k_oth, v_own, v_oth, o, do, lse, qi, ki)
+    ride_finish(rider, parts_ride)
+
+
+def attention_backward(q, keys, o, do, lse, ids, causal, rider=None):
+    outs = [jax.ShapeDtypeStruct(q.shape, BF16)] * 5
+    return attention_call(
+        attn_bwd_kernel, "attn_bwd", causal, rider, [q, *keys, o, do, lse], ids, outs
+    )
 
 
 def norm(value):
@@ -200,35 +396,38 @@
     return jnp.einsum("tpm,tkm->pk", blocks, weight, preferred_element_type=F32)
 
 
-def self_forward(rows_bf, rows, w_attn, ids, causal):
+def self_forward(rows_bf, rows, w_attn, ids, causal, rider=None):
     kv = [project(rows_bf, w_attn[:, j]).astype(BF16) for j in (1, 2)]
     other = swap(jnp.stack(kv))
     q = project(rows_bf, w_attn[:, 0]).astype(BF16)
     keys = (kv[0], other[0], kv[1], other[1])
-    o, lse = attention_forward(q, *keys, *ids[0], causal)
+    (o, lse), moved = attention_forward(q, keys, ids[0], causal, rider)
     h, rstd = norm(rows + unproject(o, w_attn[:, 3]))
-    return h, (q, keys, o, lse, h, rstd)
-
-
-def attend_back(q, keys, o, do, lse, ids, causal):
-    dq, dko, dkx, dvo, dvx = attention_backward(q, *keys, o, do, lse, *ids[1], causal)
+    return h, (q, keys, o, lse, h, rstd), moved
+
+
+def attend_back(q, keys, o, do, lse, ids, causal, rider=None):
+    (dq, dko, dkx, dvo, dvx), moved = attention_backward(
+        q, keys, o, do, lse, ids[1], causal, rider
+    )
     other = swap(jnp.stack([dkx, dvx])).astype(F32)
     dk = (dko.astype(F32) + other[0]).astype(BF16)
     dv = (dvo.astype(F32) + other[1]).astype(BF16)
-    return dq, dk, dv
-
-
-def self_backward(grad, kept, w_attn, ids, causal):
+    return (dq, dk, dv), moved
+
+
+def self_backward(grad, kept, w_attn, ids, causal, rider=None):
     q, keys, o, lse, h, rstd = kept
     dpre = norm_back(h, rstd, grad)
     do = project(dpre.astype(BF16), w_attn[:, 3]).astype(BF16)
-    dq, dk, dv = attend_back(q, keys, o, do, lse, ids, causal)
-    return (
+    (dq, dk, dv), moved = attend_back(q, keys, o, do, lse, ids, causal, rider)
+    total = (
         unproject(dq, w_attn[:, 0])
         + unproject(dk, w_attn[:, 1])
         + unproject(dv, w_attn[:, 2])
         + dpre
     )
+    return total, moved
 
 
 def tail_forward(h, tail_w):
@@ -263,28 +462,17 @@
     terms = (
         jnp.einsum("pk,tpm->tkm", rows, du, preferred_element_type=F32),
         jnp.sum(du.astype(F32), axis=1),
-        4.0 * jnp.einsum("tpm,pk->tmk", s, db, preferred_element_type=F32),
+        4.0 * jnp.einsum("pk,tpm->tkm", db, s, preferred_element_type=F32),
         4.0 * jnp.sum(db.astype(F32), axis=0),
     )
     return unproject(df, w_in) + unproject(du, a_in) + dpre, terms
-
-
-def remote(src, dst, send, recv, where):
-    return pltpu.make_async_remote_copy(
-        src_ref=src,
-        dst_ref=dst,
-        send_sem=send,
-        recv_sem=recv,
-        device_id=where,
-        device_id_type=pl.DeviceIdType.MESH,
-    )
 
 
 def gather_kernel(entry, groups, window, *refs):
     shards = refs[:groups]
-    tokens, = refs[groups : groups + 1]
-    outs = refs[groups + 1 : 2 * groups + 1]
-    placed = refs[2 * groups + 1]
+    tokens, ids = refs[groups : groups + 2]
+    outs = refs[groups + 2 : 2 * groups + 2]
+    placed, all_ids = refs[2 * groups + 2 : 2 * groups + 4]
     (
         z_send,
         z_recv,
@@ -297,9 +485,11 @@
         own_sem,
         t_send,
         t_recv,
-    ) = refs[2 * groups + 2 : 2 * groups + 13]
-    stores = refs[2 * groups + 13 : 3 * groups + 13]
-    token_store = refs[3 * groups + 13]
+        i_send,
+        i_recv,
+    ) = refs[2 * groups + 4 : 2 * groups + 17]
+    stores = refs[2 * groups + 17 : 3 * groups + 17]
+    token_store = refs[3 * groups + 17]
     s = lax.axis_index("section")
     c = lax.axis_index("ctx")
     t = lax.axis_index("tp")
@@ -326,6 +516,15 @@
         pl.semaphore_signal(barrier, 1, device_id=where, device_id_type=pl.DeviceIdType.MESH)
     pl.semaphore_wait(barrier, chips - 1 + 4)
 
+    keep_ids = pltpu.make_async_copy(ids, all_ids.at[c], i_send.at[0])
+    keep_ids.start()
+    id_copies = [
+        remote(ids, all_ids.at[c], i_send.at[j], i_recv.at[j], (s, lax.rem(c + j, 4), t))
+        for j in (1, 2, 3)
+    ]
+    for copy in id_copies:
+        copy.start()
+
     def token_copy(i):
         p = lax.rem(chip + i, chips)
         return p, remote(
@@ -439,7 +638,7 @@
         start_z(i)
     bring.wait()
     keep.start()
-    lag = LAG
+    lag = 2
     for step in range(count + 2 * lag):
         if step < count:
             stage2(step)
@@ -482,6 +681,10 @@
             got(outs[g].at[t], own_sem.at[g, 2])
 
     keep.wait()
+    keep_ids.wait()
+    for j, copy in enumerate(id_copies):
+        copy.wait_send()
+        got(all_ids.at[lax.rem(c + 3 - j, 4)], i_recv.at[j + 1])
     for i in range(1, chips):
         p, copy = token_copy(i)
         pl.when(p < rows)(copy.wait_send)
@@ -492,10 +695,7 @@
             got(region, t_recv.at[i])
 
 
-LAG = 2
-
-
-def gather_call(entry, shards, tokens, window=4):
+def gather_call(entry, shards, tokens, ids, window=4):
     groups = len(shards)
     kinds, _, part, width = tokens.shape
     dma = pltpu.SemaphoreType.DMA
@@ -512,13 +712,18 @@
         (groups, 4),
         (16,),
         (16,),
+        (4,),
+        (4,),
     ]
     result = pl.pallas_call(
         functools.partial(gather_kernel, entry, groups, window),
-        in_specs=[anywhere] * (groups + 1),
-        out_specs=[anywhere] * (groups + 1),
+        in_specs=[anywhere] * (groups + 2),
+        out_specs=[anywhere] * (groups + 2),
         out_shape=[jax.ShapeDtypeStruct((4,) + v.shape, v.dtype) for v in shards]
-        + [jax.ShapeDtypeStruct((kinds, 16, part, width), tokens.dtype)],
+        + [
+            jax.ShapeDtypeStruct((kinds, 16, part, width), tokens.dtype),
+            jax.ShapeDtypeStruct((4,) + ids.shape, ids.dtype),
+        ],
         scratch_shapes=[dma(size) for size in sizes]
         + [pltpu.VMEM(v.shape, v.dtype) for v in shards]
         + [pltpu.VMEM((kinds, part, width), tokens.dtype)],
@@ -526,8 +731,8 @@
             collective_id=entry, has_side_effects=True, vmem_limit_bytes=24 * 2**20
         ),
         name="gather_%d" % entry,
-    )(*shards, tokens)
-    return result[:groups], result[groups]
+    )(*shards, tokens, ids)
+    return result[:groups], result[groups], result[groups + 1]
 
 
 def gather_plain(entry, shards):
@@ -601,14 +806,21 @@
         cross_weights[0].reshape(-1, cross_weights.shape[3]),
         biases,
     ]
-    if lax.axis_size("ctx") == 4 and tp == 4:
-        enc_w, placed = gather_call(0, shards, stacked[:1])
+    near = lax.axis_size("ctx") == 4 and tp == 4
+    if near:
+        ids = jnp.stack([src_seg, tgt_seg]).reshape(2 * row_count, -1)
+        enc_w, placed, ids = gather_call(0, shards, stacked[:1], ids)
         source = placed.reshape(length, width)
-        dec_w, placed = gather_call(1, shards, stacked[1:])
-        target, cotangent = placed.reshape(2, length, width)
+        dec_w, placed, _ = gather_call(1, shards, stacked[1:2], ids[0])
+        target = placed.reshape(length, width)
+        flat_ids = ids.swapaxes(0, 1).reshape(2, row_count, -1)
     else:
         source, target, cotangent = spread(stacked)
         enc_w, dec_w = gather_plain(0, shards), gather_plain(1, shards)
+        flat_ids = [
+            lax.all_gather(v.reshape(row_count, -1), "ctx", axis=1, tiled=True)
+            for v in (src_seg, tgt_seg)
+        ]
 
     def unpack(full):
         attn, w_in, adapter, w_out, cross, bias = full
@@ -629,10 +841,7 @@
     enc_attn, enc_cross, enc_tail_w = unpack(enc_w)
     dec_attn, dec_cross, dec_tail_w = unpack(dec_w)
 
-    def ids_of(segments):
-        flat = lax.all_gather(
-            segments.reshape(row_count, -1), "ctx", axis=1, tiled=True
-        )
+    def ids_of(flat):
         row = lax.dynamic_index_in_dim(
             flat, jnp.minimum(chip, row_count - 1), 0, keepdims=False
         )
@@ -645,7 +854,7 @@
         own = lax.dynamic_index_in_dim(seg, which, 1, keepdims=False).reshape(length)
         return own, place + which * half
 
-    src_ids, tgt_ids = ids_of(src_seg), ids_of(tgt_seg)
+    src_ids, tgt_ids = ids_of(flat_ids[0]), ids_of(flat_ids[1])
 
     def id_arrays(seg_q, seg_k):
         qi = jnp.stack(cut(seg_q, core))
@@ -656,37 +865,92 @@
     dec_ids = id_arrays(tgt_ids, tgt_ids)
     cross_ids = id_arrays(tgt_ids, src_ids)
 
-    enc_mid, enc_self = self_forward(
-        source, source.astype(F32), enc_attn, enc_ids, False
-    )
+    def scatter(arrays, call_id):
+        return Scatter(arrays, row_count, call_id) if near else None
+
+    def tokens(value):
+        return value.astype(BF16).reshape(chips, half, width)
+
+    ride = scatter([(stacked[2], Scatter.BRING)], 6)
+    enc_mid, enc_self, moved = self_forward(
+        source, source.astype(F32), enc_attn, enc_ids, False, ride
+    )
+    if near:
+        cotangent = moved[0].reshape(length, width)
     encoded, enc_tail = tail_forward(enc_mid, enc_tail_w)
     encoded_bf = encoded.astype(BF16)
     memory = [project(encoded_bf, enc_cross[:, j]).astype(BF16) for j in range(2)]
     memory_other = swap(jnp.stack(memory))
     mem_keys = (memory[0], memory_other[0], memory[1], memory_other[1])
 
-    dec_mid, dec_self = self_forward(
+    dec_mid, dec_self, _ = self_forward(
         target, target.astype(F32), dec_attn, dec_ids, True
     )
     queries = project(dec_mid.astype(BF16), dec_cross[:, 0]).astype(BF16)
-    cross_o, cross_lse = attention_forward(
-        queries, *mem_keys, *cross_ids[0], False
+    ride = scatter([(tokens(encoded_bf), 0)], 7)
+    (cross_o, cross_lse), out_enc = attention_forward(
+        queries, mem_keys, cross_ids[0], False, ride
     )
     second, second_rstd = norm(dec_mid + unproject(cross_o, dec_cross[:, 1]))
     decoded, dec_tail = tail_forward(second, dec_tail_w)
+
+    def pieces(terms):
+        d_in, d_bias, d_out, d_last = terms
+        cuts = [v.reshape(tp, 4, width // 4, lanes).swapaxes(0, 1) for v in (d_in, d_out)]
+        tail = jnp.concatenate(
+            [
+                d_bias[:, None, :],
+                jnp.broadcast_to(d_last.reshape(1, -1, lanes), (tp, width // lanes, lanes)),
+            ],
+            axis=1,
+        )
+        tail = jnp.pad(tail, ((0, 0), (0, 16 - tail.shape[1]), (0, 0)))
+        tail = jnp.broadcast_to(tail, (4,) + tail.shape)
+        first, other = [
+            jnp.concatenate([v, tail], axis=2).reshape(4 * tp, -1, lanes) for v in cuts
+        ]
+        got = swap(pick(other, first).astype(BF16)).astype(F32)
+        return (pick(first, other) + got).astype(BF16)
 
     grad_second, dec_terms = tail_backward(cotangent.astype(F32), dec_tail, dec_tail_w)
     grad_cross = norm_back(second, second_rstd, grad_second)
     do = project(grad_cross.astype(BF16), dec_cross[:, 1]).astype(BF16)
-    dqc, dmk, dmv = attend_back(
-        queries, mem_keys, cross_o, do, cross_lse, cross_ids, False
+    ride = scatter([(tokens(decoded), 1)], 2)
+    (dqc, dmk, dmv), out_dec = attend_back(
+        queries, mem_keys, cross_o, do, cross_lse, cross_ids, False, ride
     )
     grad_first = unproject(dqc, dec_cross[:, 0]) + grad_cross
-    grad_target = self_backward(grad_first, dec_self, dec_attn, dec_ids, True)
+    ride = scatter([(pieces(dec_terms), 1)], 3) if near else None
+    grad_target, dec_sum = self_backward(
+        grad_first, dec_self, dec_attn, dec_ids, True, ride
+    )
 
     grad_encoded = unproject(dmk, enc_cross[:, 0]) + unproject(dmv, enc_cross[:, 1])
     grad_mid, enc_terms = tail_backward(grad_encoded, enc_tail, enc_tail_w)
-    grad_source = self_backward(grad_mid, enc_self, enc_attn, enc_ids, False)
+    ride = (
+        scatter([(pieces(enc_terms), 0), (tokens(grad_target), 1)], 4) if near else None
+    )
+    grad_source, moved = self_backward(
+        grad_mid, enc_self, enc_attn, enc_ids, False, ride
+    )
+
+    if near:
+        outs = pick(out_enc[0], out_dec[0])
+        sums = jnp.sum(pick(moved[0], dec_sum[0]).astype(F32), axis=0)
+        last, whole = send_call(
+            scatter([(tokens(grad_source), 0)], 5), sums[:, : width // 4].reshape(-1, lanes).astype(BF16)
+        )
+        grads = pick(last[0], moved[1]).astype(F32)
+        whole = whole.astype(F32).reshape(4, 2, width // 4, lanes).swapaxes(0, 1)
+        whole = whole.reshape(2, width, lanes)
+        return (
+            outs.reshape(layer_inputs.shape),
+            grads.reshape(layer_inputs.shape),
+            whole[0][None],
+            sums[0, width // 4][None],
+            whole[1].T[None],
+            sums[0, width // 4 + 1 : width // 4 + 1 + width // lanes].reshape(1, width),
+        )
 
     has_row = chip < row_count
 
@@ -725,7 +989,7 @@
         grads,
         scattered[0][None],
         scattered[1][None],
-        scattered[2][None],
+        scattered[2].T[None],
         bias_sum[None],
     )
 

time: 941 us -> 806 us (0.86)
  waiting for transfers between devices: 123 us -> 0.02 us
  blocking collectives: 74 us -> 0 us
  Pallas kernels: 458 us -> 506 us
  local copies, waits for them, and re-layouts: 48.8 us -> 67.4 us
  matrix products: 157 us -> 171 us
  between operations: 15.7 us -> 2.62 us
    all_to_all x1 -> x0, waiting for transfers between devices: 118 us -> none  [collect(): moved = lax.all_to_all(blocks, ('ctx', 'tp'), 0, 0, tiled=True)]
    pallas_call x6 -> x7, Pallas kernels: 153 us -> 220 us  [the longest x6 191 us: attention_call(): pl.pallas_call(functools.partial(kernel, causal, rider), grid=(groups,),...]
    psum x2 -> x0, blocking collectives: 48.1 us -> none  [the longest x1 40.6 us: per_device(): bias_sum = lax.psum(sums[3], ('ctx', 'tp')).astype(F32)]
    reshape x2 -> x9, local copies, waits for them, and re-layouts: 0.03 us -> 25 us  [the longest x8 25 us: pieces(): v.reshape(tp, 4, width // 4, lanes).swapaxes(0, 1)]
    pallas_call x2, Pallas kernels: 305 us -> 286 us  [gather_call(): pl.pallas_call(functools.partial(gather_kernel, entry, groups, window), i...]
    all_gather x2 -> x0, blocking collectives: 17.5 us -> none  [ids_of(): lax.all_gather(segments.reshape(row_count, -1), 'ctx', axis=1, tiled=True)]
    all_to_all x1 -> x0, starting transfers between devices: 13.9 us -> none  [collect(): moved = lax.all_to_all(blocks, ('ctx', 'tp'), 0, 0, tiled=True)]
    ppermute x13 -> x9, starting transfers between devices: 3.11 us -> 13.8 us  [swap(): return lax.ppermute(value, 'section', [(0, 1), (1, 0)])]
  transfers between devices with their start and end apart: 17 -> 9, of which waited for: 3 -> 0; matrix products, arithmetic and copies ran while one was open for 14% -> 20% of each run, Pallas kernels for 29% -> 10%
where the time goes in v3:
time: 806 us; the launch traced here: 800 us
  Pallas kernels  506 us (63%)
  matrix products  171 us (21%)
  local copies, waits for them, and re-layouts  67.4 us (8%)
  other arithmetic  39.1 us (5%)
  starting transfers between devices  13.8 us (2%)
    pallas_call x2, Pallas kernels, gather_call(): pl.pallas_call(functools.partial(gather_kernel, entry, groups, window), i...  286 us
    pallas_call x6, Pallas kernels, attention_call(): pl.pallas_call(functools.partial(kernel, causal, rider), grid=(groups,),...  191 us
    dot_general x16, matrix products, unproject(): return jnp.einsum('tpm,tkm->pk', blocks, weight, preferred_element_type=F32)  89.8 us
    dot_general x16, matrix products, project(): return jnp.einsum('pk,tkm->tpm', rows, weight, preferred_element_type=F32)  48.9 us
    pallas_call x1, Pallas kernels, send_call(): pl.pallas_call(functools.partial(send_kernel, rider), in_specs=[anywhere]...  28.9 us
    unnamed x205, local copies, waits for them, and re-layouts  26.8 us
    reshape x8, local copies, waits for them, and re-layouts, pieces(): v.reshape(tp, 4, width // 4, lanes).swapaxes(0, 1)  25 us
    dot_general x2, matrix products, tail_forward(): total = jnp.einsum('tpm,tmk->pk', g, w_out, preferred_element_type=F32)  18.1 us
  transfers between devices with their start and end apart: 9, of which 0 were waited for; matrix products, arithmetic and copies ran while one was open for 20% of the time, Pallas kernels for 10%

profile of v3, /device:TPU:0, one launch (start us, length us, event | category | flops | bytes accessed | tf_op | source)
XLA Modules:
  0.0 800.1 jit_solution(755335566537067995)
XLA Ops:
  7.7 139.7 %gather_0.1 = (bf16[4,4096,256]{2,1,0:T(8,128)(2,1)S(1)}, bf16[4,1024,1024]{2,1,0:T(8,128)(2,1)}, bf16[4,1024,256]{2,1,0:T(8,128)(2,1)S(1)}, bf16[4,1024,1024]{2...) custom-call(bf16[4096,256]{1,0:T(8,128)(2,1)S(1)} %bitcast.604, ...), custom_call_target="tpu_custom_call" | custom-call | tf_op jit(solution)/shard_map/gather_0/pallas_call | solution.py:718
  151.4 146.2 %gather_1.1 = (bf16[4,4096,256]{2,1,0:T(8,128)(2,1)S(1)}, bf16[4,1024,1024]{2,1,0:T(8,128)(2,1)}, bf16[4,1024,256]{2,1,0:T(8,128)(2,1)S(1)}, bf16[4,1024,1024]{2...) custom-call(bf16[4096,256]{1,0:T(8,128)(2,1)S(1)} %bitcast.605, ...), custom_call_target="tpu_custom_call" | custom-call | tf_op jit(solution)/shard_map/gather_1/pallas_call | solution.py:718
  299.0 3.2 fusion.111
  302.2 3.2 fusion.110
  317.2 4.3 fusion.113.q_ref
  324.3 3.3 slice_bitcast_fusion.94
  327.7 32.6 %attn_fwd.4 = (bf16[4,512,256]{2,1,0:T(8,128)(2,1)S(1)}, f32[4,4,512]{2,1,0:T(4,128)S(1)}, bf16[16,32,1024]{2,1,0:T(8,128)(2,1)S(1)}) custom-call(bf16[4,512,256]{2,1,0:T(8,128)(2,1)S(1)} %fusion.116.q_ref, bf16[4,512,256]{2,1,0:T(8,128)(2,1)S(1)} %bitcast.607, bf16[4,512,256]{2,1,0:T(8,128)(2,1)} %get-tuple-element.116.kx_ref, ...), custom_call_target="tpu_custom_call" | custom-call | tf_op jit(solution)/shard_map/attn_fwd/pallas_call | solution.py:282
  360.4 3.4 fusion.198
  368.2 7.4 fusion.206
  375.6 7.9 fusion.199
  394.4 21.2 %attn_fwd.3 = (bf16[4,512,256]{2,1,0:T(8,128)(2,1)S(1)}, f32[4,4,512]{2,1,0:T(4,128)S(1)}) custom-call(bf16[4,512,256]{2,1,0:T(8,128)(2,1)S(1)} %copy-done.14, bf16[4,512,256]{2,1,0:T(8,128)(2,1)S(1)} %bitcast.617, bf16[4,512,256]{2,1,0:T(8,128)(2,1)S(1)} %get-tuple-element.118.kx_ref, bf16[4,512,256]{2,1,0:T(8,128)(2,1)S(1)} %bitcast.620, ...), custom_call_target="tpu_custom_call" | custom-call | tf_op jit(solution)/shard_map/attn_fwd/pallas_call | solution.py:282
  415.6 3.6 fusion.197
  424.0 28.9 %attn_fwd.5 = (bf16[4,512,256]{2,1,0:T(8,128)(2,1)S(1)}, f32[4,4,512]{2,1,0:T(4,128)S(1)}, bf16[12,2,32,1024]{3,2,1,0:T(8,128)(2,1)}) custom-call(bf16[4,512,256]{2,1,0:T(8,128)(2,1)S(1)} %fusion.115.q_ref, bf16[4,512,256]{2,1,0:T(8,128)(2,1)S(1)} %bitcast.610, bf16[4,512,256]{2,1,0:T(8,128)(2,1)S(1)} %get-tuple-element.114.kx_ref, ...), custom_call_target="tpu_custom_call" | custom-call | tf_op jit(solution)/shard_map/attn_fwd/pallas_call | solution.py:282
  458.6 7.2 fusion.207
  465.8 10.2 %fusion.201 = (f32[512]{0:T(512)S(1)}, f32[512,1024]{1,0:T(8,128)S(1)}) fusion(f32[1024]{0:T(1024)S(1)} %copy-done.82, f32[512,1024,1]{1,0,2:T(8,128)S(1)} %fusion.159, bf16[4,1024,1024]{2,1,0:T(8,128)(2,1)} %get-tuple-element.65, f32[4,1024,512]{2,1,0:T(8,128)} %fusion.207, f32[512]{0:T(512)S(1)} %add_rsqrt_fusion.1, ...), kind=kOutput, calls=%fused_computation.334 | convolution fusion | flops 4309122560 | bytes 23078912 | tf_op jit(solution)/shard_map/tpm,tmk->pk/dot_general | solution.py:444
  486.0 28.5 %fusion.193 = (f32[512]{0:T(512)S(1)}, f32[512]{0:T(512)S(1)}, f32[512,1024]{1,0:T(8,128)}) fusion(f32[512]{0:T(512)S(1)} %copy-done.81, f32[512,1024]{1,0:T(8,128)S(1)} %copy-done.54, f32[512]{0:T(512)S(1)} %broadcast_multiply_fusion.11, f32[512,1024]{1,0:T(8,128)} %copy-done.67, f32[512,1024,1]{1,0,2:T(8,128)} %fusion.161, ...), kind=kOutput, calls=%fused_computation.327 | convolution fusion | flops 8619294720 | bytes 33562624 | tf_op jit(solution)/shard_map/tpm,tkm->pk/dot_general | solution.py:396
  514.5 4.7 fusion.118.do_ref
  519.2 37.2 %attn_bwd.3 = (bf16[4,512,256]{2,1,0:T(8,128)(2,1)S(1)}, bf16[4,512,256]{2,1,0:T(8,128)(2,1)S(1)}, bf16[4,512,256]{2,1,0:T(8,128)(2,1)S(1)}, bf16[4,512,256]{2,1...) custom-call(bf16[4,512,256]{2,1,0:T(8,128)(2,1)} %copy-done.13, ...), custom_call_target="tpu_custom_call" | custom-call | tf_op jit(solution)/shard_map/attn_bwd/pallas_call | solution.py:282
  562.8 3.2 reshape.338
  568.9 3.2 reshape.339
  572.0 3.4 copy.205
  580.5 4.0 fusion.114.do_ref
  585.7 28.4 %attn_bwd.4 = (bf16[4,512,256]{2,1,0:T(8,128)(2,1)S(1)}, bf16[4,512,256]{2,1,0:T(8,128)(2,1)S(1)}, bf16[4,512,256]{2,1,0:T(8,128)(2,1)S(1)}, bf16[4,512,256]{2,1...) custom-call(bf16[4,512,256]{2,1,0:T(8,128)(2,1)} %fusion.113.q_ref, ...), custom_call_target="tpu_custom_call" | custom-call | tf_op jit(solution)/shard_map/attn_bwd/pallas_call | solution.py:282
  617.0 4.2 fusion.67
  634.0 29.1 %fusion.191 = (f32[512]{0:T(512)S(1)}, f32[512]{0:T(512)S(1)}, f32[512,1024]{1,0:T(8,128)}) fusion(f32[512]{0:T(512)S(1)} %add_rsqrt_fusion.3, f32[512,1024]{1,0:T(8,128)} %copy-done.42, f32[512]{0:T(512)S(1)} %broadcast_multiply_fusion.13, f32[512,1024]{1,0:T(8,128)} %copy-done.66, f32[512,1024,1]{1,0,2:T(8,128)} %fusion.167, ...), kind=kOutput, calls=%fused_computation.325 | convolution fusion | flops 8619294720 | bytes 33562624 | tf_op jit(solution)/shard_map/tpm,tkm->pk/dot_general | solution.py:396
  666.2 3.2 reshape.336
  672.3 3.7 multiply_bitcast_fusion.1
  676.0 3.2 reshape.337
  687.3 4.2 fusion.117.do_ref
  700.5 42.6 %attn_bwd.5 = (bf16[4,512,256]{2,1,0:T(8,128)(2,1)S(1)}, bf16[4,512,256]{2,1,0:T(8,128)(2,1)S(1)}, bf16[4,512,256]{2,1,0:T(8,128)(2,1)S(1)}, bf16[4,512,256]{2,1...) custom-call(bf16[4,512,256]{2,1,0:T(8,128)(2,1)} %copy-done.12, ...), custom_call_target="tpu_custom_call" | custom-call | tf_op jit(solution)/shard_map/attn_bwd/pallas_call | solution.py:282
  743.3 11.1 %collective-permute-start.8 = (bf16[2,4,512,256]{3,2,1,0:T(8,128)(2,1)S(1)}, bf16[2,4,512,256]{3,2,1,0:T(8,128)(2,1)S(1)}, u32[]{:S(2)}, u32[]{:S(2)}) collective-permute-start(bf16[2,4,512,256]{3,2,1,0:T(8,128)(2,1)S(1)} %pad_maximum_fusion.10), channel_id=1, source_target_pairs={{0,16},{16,0},{1,17},{17,1},{2,18},{18,2},{3,19},{19,3},{4,20},{20... | collective-permute-start | bytes 6291464 | tf_op jit(solution)/shard_map/ppermute | solution.py:19
  765.2 28.9 %send_last.1 = (bf16[12,2,32,1024]{3,2,1,0:T(8,128)(2,1)}, bf16[4,512,128]{2,1,0:T(8,128)(2,1)}) custom-call(bf16[16,32,1024]{2,1,0:T(8,128)(2,1)} %bitcast.688, bf16[512,128]{1,0:T(8,128)(2,1)} %bitcast.698), custom_call_target="tpu_custom_call" | custom-call | tf_op jit(solution)/shard_map/send_last/pallas_call | solution.py:198
  (359 shorter events, 132.4 us)
Async XLA Ops:
  2.3 2.7 collective-permute-start
  151.4 155.3 %copy-start.23 = (bf16[4,4096,256]{2,1,0:T(8,128)(2,1)}, bf16[4,4096,256]{2,1,0:T(8,128)(2,1)S(1)}, u32[]{:S(2)}) copy-start(bf16[4,4096,256]{2,1,0:T(8,128)(2,1)S(1)} %get-tuple-element.57) | copy-start | bytes 25165828
  151.4 155.3 %copy-start.36 = (bf16[1,16,32,1024]{3,2,1,0:T(8,128)(2,1)}, bf16[1,16,32,1024]{3,2,1,0:T(8,128)(2,1)S(1)}, u32[]{:S(2)}) copy-start(bf16[1,16,32,1024]{3,2,1,0:T(8,128)(2,1)S(1)} %get-tuple-element.56) | copy-start | bytes 3145732
  306.8 20.9 %copy-start = (bf16[4,256,512]{1,2,0:T(8,128)(2,1)}, bf16[4,256,512]{1,2,0:T(8,128)(2,1)S(1)}, u32[]{:S(2)}) copy-start(bf16[4,256,512]{1,2,0:T(8,128)(2,1)S(1)} %fusion.106) | copy-start | bytes 3145732
  309.7 14.6 %collective-permute-start.2 = (bf16[2,4,512,256]{3,2,1,0:T(8,128)(2,1)}, bf16[2,4,512,256]{3,2,1,0:T(8,128)(2,1)}, u32[]{:S(2)}, u32[]{:S(2)}) collective-permute-start(bf16[2,4,512,256]{3,2,1,0:T(8,128)(2,1)} %pad_maximum_fusion.6), channel_id=1, source_target_pairs={{0,16},{16,0},{1,17},{17,1},{2,18},{18,2},{3,19},{19,3},{4,20},{20... | collective-permute-start | bytes 6291464 | tf_op jit(solution)/shard_map/ppermute | solution.py:19
  311.4 80.1 %collective-permute-start.1 = (bf16[2,4,512,256]{3,2,1,0:T(8,128)(2,1)}, bf16[2,4,512,256]{3,2,1,0:T(8,128)(2,1)}, u32[]{:S(2)}, u32[]{:S(2)}) collective-permute-start(bf16[2,4,512,256]{3,2,1,0:T(8,128)(2,1)} %pad_maximum_fusion.5), channel_id=1, source_target_pairs={{0,16},{16,0},{1,17},{17,1},{2,18},{18,2},{3,19},{19,3},{4,20},{20... | collective-permute-start | bytes 6291464 | tf_op jit(solution)/shard_map/ppermute | solution.py:19
  360.4 7.9 slice-start.4
  363.7 11.9 %copy-start.42 = (f32[512,1024]{1,0:T(8,128)}, f32[512,1024]{1,0:T(8,128)S(1)}, u32[]{:S(2)}) copy-start(f32[512,1024]{1,0:T(8,128)S(1)} %get-tuple-element.130) | copy-start | bytes 6291460
  367.2 8.4 %slice-start.6 = ((s8[8388608]{0:T(1024)(128)(4,1)}), s8[4194304]{0:T(1024)(128)(4,1)S(1)}, s32[]{:S(2)}) async-start(s8[8388608]{0:T(1024)(128)(4,1)} %bitcast.716), calls=%async_computation.6 | async-start | bytes 8388608
  388.2 35.9 %copy-start.1 = (bf16[4,256,512]{1,2,0:T(8,128)(2,1)}, bf16[4,256,512]{1,2,0:T(8,128)(2,1)S(1)}, u32[]{:S(2)}) copy-start(bf16[4,256,512]{1,2,0:T(8,128)(2,1)S(1)} %fusion.103) | copy-start | bytes 3145732
  389.4 34.6 %copy-start.2 = (bf16[4,256,512]{1,2,0:T(8,128)(2,1)}, bf16[4,256,512]{1,2,0:T(8,128)(2,1)S(1)}, u32[]{:S(2)}) copy-start(bf16[4,256,512]{1,2,0:T(8,128)(2,1)S(1)} %fusion.102) | copy-start | bytes 3145732
  391.1 29.8 %collective-permute-start.3 = (bf16[2,4,512,256]{3,2,1,0:T(8,128)(2,1)}, bf16[2,4,512,256]{3,2,1,0:T(8,128)(2,1)}, u32[]{:S(2)}, u32[]{:S(2)}) collective-permute-start(bf16[2,4,512,256]{3,2,1,0:T(8,128)(2,1)} %pad_maximum_fusion.7), channel_id=1, source_target_pairs={{0,16},{16,0},{1,17},{17,1},{2,18},{18,2},{3,19},{19,3},{4,20},{20... | collective-permute-start | bytes 6291464 | tf_op jit(solution)/shard_map/ppermute | solution.py:19
  394.4 21.2 %copy-start.8 = (bf16[4,512,256]{2,1,0:T(8,128)(2,1)}, bf16[4,512,256]{2,1,0:T(8,128)(2,1)S(1)}, u32[]{:S(2)}) copy-start(bf16[4,512,256]{2,1,0:T(8,128)(2,1)S(1)} %get-tuple-element.118.kx_ref) | copy-start | bytes 3145732
  419.3 33.7 %copy-start.49 = (f32[512,1024]{1,0:T(8,128)}, f32[512,1024]{1,0:T(8,128)S(1)}, u32[]{:S(2)}) copy-start(f32[512,1024]{1,0:T(8,128)S(1)} %get-tuple-element.128) | copy-start | bytes 6291460
  424.0 29.0 %copy-start.3 = (bf16[4,512,256]{2,1,0:T(8,128)(2,1)}, bf16[4,512,256]{2,1,0:T(8,128)(2,1)S(1)}, u32[]{:S(2)}) copy-start(bf16[4,512,256]{2,1,0:T(8,128)(2,1)S(1)} %get-tuple-element.114.kx_ref) | copy-start | bytes 3145732
  454.4 11.4 %copy-start.53 = (f32[512,1024]{1,0:T(8,128)}, f32[512,1024]{1,0:T(8,128)S(1)}, u32[]{:S(2)}) copy-start(f32[512,1024]{1,0:T(8,128)S(1)} %get-tuple-element.134) | copy-start | bytes 6291460
  454.8 11.0 %copy-start.80 = (f32[512]{0:T(512)}, f32[512]{0:T(512)S(1)}, u32[]{:S(2)}) copy-start(f32[512]{0:T(512)S(1)} %add_rsqrt_fusion.1) | copy-start | bytes 6148
  519.2 39.0 %copy-start.50 = (f32[512,1024]{1,0:T(8,128)S(1)}, f32[512,1024]{1,0:T(8,128)}, u32[]{:S(2)}) copy-start(f32[512,1024]{1,0:T(8,128)} %copy-done.49) | copy-start | bytes 6291460
  519.2 39.0 %copy-start.55 = (f32[512,1024]{1,0:T(8,128)S(1)}, f32[512,1024]{1,0:T(8,128)}, u32[]{:S(2)}) copy-start(f32[512,1024]{1,0:T(8,128)} %copy-done.53) | copy-start | bytes 6291460
  519.2 39.0 %copy-start.86 = (f32[512,1024]{1,0:T(8,128)S(1)}, f32[512,1024]{1,0:T(8,128)}, u32[]{:S(2)}) copy-start(f32[512,1024]{1,0:T(8,128)} %get-tuple-element.137) | copy-start | bytes 6291460
  558.1 63.1 %collective-permute-start.4 = (bf16[2,4,512,256]{3,2,1,0:T(8,128)(2,1)}, bf16[2,4,512,256]{3,2,1,0:T(8,128)(2,1)}, u32[]{:S(2)}, u32[]{:S(2)}) collective-permute-start(bf16[2,4,512,256]{3,2,1,0:T(8,128)(2,1)} %pad_maximum_fusion.8), channel_id=1, source_target_pairs={{0,16},{16,0},{1,17},{17,1},{2,18},{18,2},{3,19},{19,3},{4,20},{20... | collective-permute-start | bytes 6291464 | tf_op jit(solution)/shard_map/ppermute | solution.py:19
  578.1 6.4 collective-permute-start.6
  615.6 75.9 %collective-permute-start.7 = (bf16[2,4,512,256]{3,2,1,0:T(8,128)(2,1)}, bf16[2,4,512,256]{3,2,1,0:T(8,128)(2,1)}, u32[]{:S(2)}, u32[]{:S(2)}) collective-permute-start(bf16[2,4,512,256]{3,2,1,0:T(8,128)(2,1)} %pad_maximum_fusion.9), channel_id=1, source_target_pairs={{0,16},{16,0},{1,17},{17,1},{2,18},{18,2},{3,19},{19,3},{4,20},{20... | collective-permute-start | bytes 6291464 | tf_op jit(solution)/shard_map/ppermute | solution.py:19
  634.0 29.1 %copy-start.58 = (bf16[512,1024,1]{1,0,2:T(8,128)(2,1)S(1)}, bf16[512,1024,1]{1,0,2:T(8,128)(2,1)}, u32[]{:S(2)}) copy-start(bf16[512,1024,1]{1,0,2:T(8,128)(2,1)} %copy-done.57) | copy-start | bytes 3145732
  685.0 14.3 %collective-permute-start.5 = (bf16[16,272,128]{2,1,0:T(8,128)(2,1)S(1)}, bf16[16,272,128]{2,1,0:T(8,128)(2,1)S(1)}, u32[]{:S(2)}, u32[]{:S(2)}) collective-permute-start(bf16[16,272,128]{2,1,0:T(8,128)(2,1)S(1)} %bitcast.694), channel_id=1, source_target_pairs={{0,16},{16,0},{1,17},{17,1},{2,18},{18,2},{3,19},{19,3},{4,20},{20... | collective-permute-start | bytes 3342344 | tf_op jit(solution)/shard_map/ppermute | solution.py:19
  685.8 7.7 slice-start.2
  700.5 53.9 %copy-start.70 = (bf16[12,2,32,1024]{3,2,1,0:T(8,128)(2,1)S(1)}, bf16[12,2,32,1024]{3,2,1,0:T(8,128)(2,1)}, u32[]{:S(2)}) copy-start(bf16[12,2,32,1024]{3,2,1,0:T(8,128)(2,1)} %get-tuple-element.63) | copy-start | bytes 4718596
  700.5 53.9 %copy-start.71 = (bf16[12,2,32,1024]{3,2,1,0:T(8,128)(2,1)S(1)}, bf16[12,2,32,1024]{3,2,1,0:T(8,128)(2,1)}, u32[]{:S(2)}) copy-start(bf16[12,2,32,1024]{3,2,1,0:T(8,128)(2,1)} %get-tuple-element.71) | copy-start | bytes 4718596
  700.5 58.7 %slice-start = ((s8[8388608]{0:T(1024)(128)(4,1)}), s8[4194304]{0:T(1024)(128)(4,1)S(1)}, s32[]{:S(2)}) async-start(s8[8388608]{0:T(1024)(128)(4,1)} %bitcast.648), calls=%async_computation | async-start | bytes 8388608
  743.1 16.0 %slice-start.1 = ((s8[8388608]{0:T(1024)(128)(4,1)}), s8[4194304]{0:T(1024)(128)(4,1)S(1)}, s32[]{:S(2)}) async-start(s8[8388608]{0:T(1024)(128)(4,1)} %bitcast.648), calls=%async_computation.1 | async-start | bytes 8388608
  743.3 17.1 %collective-permute-start.8 = (bf16[2,4,512,256]{3,2,1,0:T(8,128)(2,1)S(1)}, bf16[2,4,512,256]{3,2,1,0:T(8,128)(2,1)S(1)}, u32[]{:S(2)}, u32[]{:S(2)}) collective-permute-start(bf16[2,4,512,256]{3,2,1,0:T(8,128)(2,1)S(1)} %pad_maximum_fusion.10), channel_id=1, source_target_pairs={{0,16},{16,0},{1,17},{17,1},{2,18},{18,2},{3,19},{19,3},{4,20},{20... | collective-permute-start | bytes 6291464 | tf_op jit(solution)/shard_map/ppermute | solution.py:19
  762.4 31.7 %copy-start.72 = (bf16[12,2,32,1024]{3,2,1,0:T(8,128)(2,1)S(1)}, bf16[12,2,32,1024]{3,2,1,0:T(8,128)(2,1)}, u32[]{:S(2)}) copy-start(bf16[12,2,32,1024]{3,2,1,0:T(8,128)(2,1)} %get-tuple-element.92) | copy-start | bytes 4718596
  (77 other events, 216.8 us)
